TPU v7x, 32 devices: a whole 2x2x4 slice. The times are simulated.
32 devices in a mesh: group: 2 (over y), tensor: 4 (over z), example: 4 (over x, core).
Axes of the slice: x: 2, y: 2, z: 4, core: 2. Of those that a mesh axis runs over, the one named last changes fastest.
Arguments:
- layer_input: bfloat16 [32, 128, 8192], P(('group', 'example'), None, 'tensor'), parts along dimension 0, may hold values from -6 to 6
- gate_pre: bfloat16 [32, 128, 28672], P(('group', 'example'), None, 'tensor'), parts along dimension 0, may hold values from -7 to 7
- up_pre: bfloat16 [32, 128, 28672], P(('group', 'example'), None, 'tensor'), parts along dimension 0, may hold values from -6 to 6
- output_grad: bfloat16 [32, 128, 8192], P(('group', 'example'), None, 'tensor'), parts along dimension 0, may hold values from -6 to 6
- down_weight: bfloat16 [28672, 8192], P('tensor', 'example'), may hold values from -0.03125 to 0.03125
- proj_input: bfloat16 [64, 8192], P(None, 'tensor'), may hold values from -0.0625 to 0.0625
- proj_hidden: bfloat16 [64, 28672], P(None, 'tensor'), may hold values from -0.03125 to 0.03125
- proj_output: bfloat16 [64, 8192], P(None, 'tensor'), may hold values from -0.0625 to 0.0625
- proj_gate: bfloat16 [64, 28672], P(None, 'tensor'), may hold values from -0.03125 to 0.03125
- proj_up: bfloat16 [64, 28672], P(None, 'tensor'), may hold values from -0.03125 to 0.03125
- query_sketches: bfloat16 [2048, 12288], P(('group', 'example'), 'tensor'), parts along dimension 0, may hold values from -6 to 6
- rev_lengths: int32 [32], P(('group', 'example')), parts along dimension 0, may hold values from 1 to 128, 1280 in all
- rev_slot: int32 [32], P('group'), parts along dimension 0, may hold values from 0 to 15, each once
- query_slot: int32 [2048], P(('group', 'example')), parts along dimension 0, may hold values from 0 to 1023, each once
Outputs:
- scores: float32 [16, 512], P('group', 'example'), parts along dimension 0
There are 2 independent parts, one for each index of `group`. A program takes and returns all parts, laid end to end along the dimension named above; an argument that names none is the same for every part. Nothing has to cross between parts.
Inputs may be any that keep to these rules, and one draw needn't show every extreme that they name: `rev_lengths`: some revision example has length exactly 128. `rev_slot`: A permutation of the revision examples' slots. `query_slot`: A permutation of the query examples' slots.
All inputs are finite; a program needn't handle non-finite values. No bound on the sum of `rev_lengths` on one device may be relied on, other than what follows from the above.
Results may differ from a plain program's by a relative error of at most 0.0035.
Values may be sent and summed in bfloat16 or wider, within the bound.
No kernel may reach another device: no remote copies, remote signals or barrier semaphores. Data moves between devices by JAX's collectives and lax.ppermute only.
A program may use at most 384 MiB of HBM per device.

v0:
```python
import functools

import jax
import jax.numpy as jnp
from jax import lax
from jax.experimental import pallas as pl
from jax.experimental.pallas import tpu as pltpu
from jax.sharding import PartitionSpec as P

LEVELS = (768,)
TILE = 512
STEP = 256
LANES = 128
VMEM_LIMIT = 58 * 1024 * 1024


def contract(left_side, right_side):
    return lax.dot_general(
        left_side, right_side, (((1,), (1,)), ((), ())), preferred_element_type=jnp.float32
    )


def contract_exact(left_side, right_side):
    return lax.dot_general(
        left_side,
        right_side,
        (((1,), (1,)), ((), ())),
        precision=lax.Precision.HIGHEST,
        preferred_element_type=jnp.float32,
    )


def pairing_table(slots, pairs):
    pair_index = slots // 2
    signs = (1 - 2 * (slots % 2)).astype(jnp.float32)
    targets = jnp.arange(pairs, dtype=jnp.int32)
    return jnp.where(targets[:, None] == pair_index[None, :], signs[None, :], jnp.float32(0.0))


def take(array, start, size, axis):
    return lax.dynamic_slice_in_dim(array, start, size, axis)


def swap(array, axis, bits):
    count = lax.axis_size(axis)
    return lax.ppermute(array, axis, [(i, i ^ bits) for i in range(count)])


def chain_pairs(rule):
    pairs = []
    for t in range(4):
        for e in range(4):
            goal = rule(3 - t if e // 2 else t, e // 2, e % 2)
            if goal is not None:
                order, far, near = goal
                pairs.append((t * 4 + e, (3 - order if far else order) * 4 + 2 * far + near))
    return pairs


CROSS = chain_pairs(lambda order, far, near: (3 - order, 1 - far, near) if order >= 2 else None)
SPREAD = chain_pairs(lambda order, far, near: (order + 2, far, near) if order < 2 else None)


def move(array, pairs):
    return lax.ppermute(array, ("tensor", "example"), pairs)


def kernel_params():
    return pltpu.CompilerParams(vmem_limit_bytes=VMEM_LIMIT)


def pack_kernel(size, count, near_ref, place_ref, own_ref, other_ref, *refs):
    outs, select = refs[-1 - count : -1], refs[-1]
    rows_own = own_ref.shape[0]

    @pl.when(pl.program_id(0) == 0)
    def _():
        @pl.loop(0, count)
        def _(c):
            at = lax.broadcasted_iota(jnp.int32, (size, select.shape[1]), 0) + c * 2 * LANES
            chosen = jnp.where(at == place_ref[...], 1.0, 0.0).astype(jnp.bfloat16)
            select[pl.ds(pl.multiple_of(c * size, size), size), :] = chosen

    for c in range(count):
        rows = slice(c * size, (c + 1) * size)
        total = jnp.dot(select[rows, :rows_own], own_ref[...], preferred_element_type=jnp.float32)
        total += jnp.dot(select[rows, rows_own:], other_ref[...], preferred_element_type=jnp.float32)
        outs[c][...] = total.astype(jnp.bfloat16).T


def pack(count, size, columns, near_offset, place, own, other, after=()):
    rows = own.shape[0]
    total = count * size
    return pl.pallas_call(
        functools.partial(pack_kernel, size, count),
        grid_spec=pltpu.PrefetchScalarGridSpec(
            num_scalar_prefetch=1,
            grid=(columns // TILE,),
            in_specs=[
                pl.BlockSpec((1, 2 * rows), lambda i, near: (0, 0)),
                pl.BlockSpec((rows, TILE), lambda i, near: (0, near[0] + i)),
                pl.BlockSpec((rows, TILE), lambda i, near: (0, near[0] + i)),
            ]
            + [pl.BlockSpec(memory_space=pl.ANY)] * len(after),
            out_specs=[pl.BlockSpec((TILE, size), lambda i, near: (i, 0))] * count,
            scratch_shapes=[pltpu.VMEM((total, 2 * rows), jnp.bfloat16)],
        ),
        out_shape=[jax.ShapeDtypeStruct((columns, size), jnp.bfloat16)] * count,
        compiler_params=kernel_params(),
        cost_estimate=pl.CostEstimate(
            flops=4 * total * rows * columns,
            bytes_accessed=(4 * rows + 2 * total) * columns,
            transcendentals=0,
        ),
        name="pack_rows",
    )(near_offset, place, own, other, *after)


def cut_kernel(at_ref, source, *refs):
    refs[-1][...] = source[...]


def cut(at, gathered, after):
    columns, rows = gathered.shape
    block = columns // 8
    return pl.pallas_call(
        cut_kernel,
        grid_spec=pltpu.PrefetchScalarGridSpec(
            num_scalar_prefetch=1,
            grid=(4,),
            in_specs=[pl.BlockSpec((block, rows), lambda i, at: (4 * at[0] + i, 0))]
            + [pl.BlockSpec(memory_space=pl.ANY)] * len(after),
            out_specs=pl.BlockSpec((block, rows), lambda i, at: (i, 0)),
        ),
        out_shape=jax.ShapeDtypeStruct((columns // 2, rows), gathered.dtype),
        compiler_params=kernel_params(),
        cost_estimate=pl.CostEstimate(flops=0, bytes_accessed=2 * columns * rows, transcendentals=0),
        name="cut_columns",
    )(at, gathered, *after)


def gate_kernel(value, *refs):
    refs[-1][...] = value[...]


def ordered(value, after):
    return pl.pallas_call(
        gate_kernel,
        in_specs=[pl.BlockSpec(memory_space=pltpu.VMEM)]
        + [pl.BlockSpec(memory_space=pl.ANY)] * len(after),
        out_specs=pl.BlockSpec(memory_space=pltpu.VMEM),
        out_shape=jax.ShapeDtypeStruct(value.shape, value.dtype),
        compiler_params=kernel_params(),
        name="ordered_copy",
    )(value, *after)


def sum_kernel(a, b, c, d, *refs):
    refs[-1][...] = (a[...] + b[...]) + (c[...] + d[...])


def sum_parts(parts, after):
    return pl.pallas_call(
        sum_kernel,
        in_specs=[pl.BlockSpec(memory_space=pltpu.VMEM)] * 4
        + [pl.BlockSpec(memory_space=pl.ANY)] * len(after),
        out_specs=pl.BlockSpec(memory_space=pltpu.VMEM),
        out_shape=jax.ShapeDtypeStruct(parts[0].shape, parts[0].dtype),
        compiler_params=kernel_params(),
        name="sum_parts",
    )(*parts, *after)


def join_kernel(at_ref, a, b, c, d, *refs):
    out = refs[-1]
    size = a.shape[1]
    for bits, part in enumerate((a, b, c, d)):
        begin = pl.multiple_of((at_ref[0] ^ bits) * size, size)
        out[:, pl.ds(begin, size)] = part[...]


def join_parts(at, parts, after):
    rows, size = parts[0].shape
    return pl.pallas_call(
        join_kernel,
        in_specs=[pl.BlockSpec(memory_space=pltpu.SMEM)]
        + [pl.BlockSpec(memory_space=pltpu.VMEM)] * 4
        + [pl.BlockSpec(memory_space=pl.ANY)] * len(after),
        out_specs=pl.BlockSpec(memory_space=pltpu.VMEM),
        out_shape=jax.ShapeDtypeStruct((rows, 4 * size), parts[0].dtype),
        compiler_params=kernel_params(),
        name="join_parts",
    )(at, *parts, *after)


def halves_kernel(a, b, *refs):
    keep, send = refs[-2:]
    half = a.shape[0] // 2
    keep[:half, :], keep[half:, :] = a[:half, :], b[:half, :]
    send[:half, :], send[half:, :] = a[half:, :], b[half:, :]


def pair_halves(a, b, after):
    shape = jax.ShapeDtypeStruct(a.shape, a.dtype)
    return pl.pallas_call(
        halves_kernel,
        in_specs=[pl.BlockSpec(memory_space=pltpu.VMEM)] * 2
        + [pl.BlockSpec(memory_space=pl.ANY)] * len(after),
        out_specs=[pl.BlockSpec(memory_space=pltpu.VMEM)] * 2,
        out_shape=[shape, shape],
        compiler_params=kernel_params(),
        name="pair_halves",
    )(a, b, *after)


def stage_kernel(far, own, offset_ref, near_ref, *refs):
    refs = list(refs)
    weights = [refs.pop(0) for _ in range(4)]
    far_ins = [refs.pop(0) for _ in range(8 * far)]
    own_ins = [refs.pop(0) for _ in range(8 * own)]
    extra = [refs.pop(0) for _ in range(5 * own)]
    own_right = refs.pop() if own else None
    far_right = refs.pop() if far else None
    out = refs.pop() if own else None
    far_out = refs.pop() if far else None
    depth = weights[0].shape[1]

    def join(ins, right):
        for block in range(4):
            for k in range(2):
                right[block * depth : (block + 1) * depth, k * LANES : (k + 1) * LANES] = ins[2 * block + k][...]

    def half_sum(rows, right):
        total = 0.0
        for k in range(4):
            block = right[k * depth : (k + 1) * depth, :]
            total += jnp.dot(weights[k][rows, :], block, preferred_element_type=jnp.float32)
        return total

    @pl.when(pl.program_id(0) == 0)
    def _():
        if far:
            join(far_ins, far_right)
        if own:
            join(own_ins, own_right)
            out[...] = jnp.zeros_like(out)

    @pl.loop(0, TILE // STEP)
    def _(r):
        rows = pl.ds(pl.multiple_of(r * STEP, STEP), STEP)
        if far:
            far_out[rows, :] = half_sum(rows, far_right).astype(jnp.bfloat16)
        if own:
            came, gate_ref, up_ref, proj_gate, proj_up = extra
            rank_size = proj_gate.shape[0]
            total = half_sum(rows, own_right)
            hidden_grad = (total + came[rows, :].astype(jnp.float32)).astype(jnp.bfloat16)
            hidden_grad = hidden_grad.astype(jnp.float32)
            gate = gate_ref[rows, :].astype(jnp.float32)
            up = up_ref[rows, :].astype(jnp.float32)
            sigma = jax.nn.sigmoid(gate)
            grad_up = (hidden_grad * (gate * sigma)).astype(jnp.bfloat16)
            grad_gate = (hidden_grad * up * sigma * (1.0 + gate * (1.0 - sigma))).astype(jnp.bfloat16)
            out[:rank_size, :] += jnp.dot(proj_gate[:, rows], grad_gate, preferred_element_type=jnp.float32)
            out[rank_size:, :] += jnp.dot(proj_up[:, rows], grad_up, preferred_element_type=jnp.float32)


def side_of(near, side):
    return near[0] + side * (1 - 2 * near[0])


def in_half(side, part, near):
    return 2 * side_of(near, side) + part


def in_whole(side, part, near):
    return 4 * near[1] + 2 * side_of(near, side) + part


def in_spread(rows, side, part, near):
    half = near[1] + part * (1 - 2 * near[1])
    return 4 * half + 2 * side_of(near, side) + rows


def stage(near_offset, near, tiles, far, own, weight, weight_near, after):
    begin, count = tiles
    width = weight_near.shape[1]
    depth = width // 2
    both = 2 * LANES
    arrays, specs, outs, shapes, rights = [], [], [], [], []

    def add(array, block, index):
        arrays.append(array)
        specs.append(pl.BlockSpec(block, index))

    for k in range(2):
        add(weight, (TILE, depth), lambda i, offset, near, k=k: (offset[0] + begin + i, k))
    for k in range(2):
        add(weight_near, (TILE, depth), lambda i, offset, near, k=k: (offset[0] + begin + i, k))
    for rows in (far, own):
        if rows is not None:
            rights.append(pltpu.VMEM((2 * width, both), jnp.bfloat16))
            for block in range(4):
                for k in range(2):
                    index = functools.partial(rows[2], *divmod(block, 2))
                    add(rows[k], (depth, LANES), lambda i, offset, near, index=index: (index(near), 0))
    if far is not None:
        outs.append(pl.BlockSpec((TILE, both), lambda i, offset, near: (i, 0)))
        shapes.append(jax.ShapeDtypeStruct((count * TILE, both), jnp.bfloat16))
    if own is not None:
        (came, first), gate, up, proj_gate, proj_up = own[3:]
        rank_size = proj_gate.shape[0]
        add(came, (TILE, both), lambda i, offset, near: (begin - first + i, 0))
        for array in (gate, up):
            add(array, (TILE, both), lambda i, offset, near: (begin + i, 0))
        for array in (proj_gate, proj_up):
            add(array, (rank_size, TILE), lambda i, offset, near: (0, offset[0] + begin + i))
        outs.append(pl.BlockSpec((2 * rank_size, both), lambda i, offset, near: (0, 0)))
        shapes.append(jax.ShapeDtypeStruct((2 * rank_size, both), jnp.float32))
    parts = len(rights)
    return pl.pallas_call(
        functools.partial(stage_kernel, far is not None, own is not None),
        grid_spec=pltpu.PrefetchScalarGridSpec(
            num_scalar_prefetch=2,
            grid=(count,),
            in_specs=specs + [pl.BlockSpec(memory_space=pl.ANY)] * len(after),
            out_specs=outs,
            scratch_shapes=rights,
        ),
        out_shape=shapes,
        compiler_params=kernel_params(),
        cost_estimate=pl.CostEstimate(
            flops=4 * parts * both * width * count * TILE,
            bytes_accessed=4 * width * count * TILE + 4 * parts * both * count * TILE,
            transcendentals=0,
        ),
        name="stage",
    )(near_offset, near, *arrays, *after)


def sum_over(array, axis):
    parts = [swap(array, axis, bits) for bits in (1, 2, 3)]
    return (array + parts[0]) + (parts[1] + parts[2])


def scatter_over(array, axis, dim):
    at = lax.axis_index(axis)
    size = array.shape[dim] // 4
    parts = [swap(take(array, (at ^ bits) * size, size, dim), axis, bits) for bits in (1, 2, 3)]
    return (take(array, at * size, size, dim) + parts[0]) + (parts[1] + parts[2])


def packed_scores(capacity, args):
    (
        layer_input,
        gate_pre,
        up_pre,
        grad_rows,
        blocks,
        place,
        down_weight,
        proj_input,
        proj_hidden,
        proj_output,
        proj_gate,
        proj_up,
        rev_slot,
        own_lengths,
    ) = args
    ex_count, slot_len, width_local = layer_input.shape
    hidden_local = gate_pre.shape[2]
    row_total = ex_count * slot_len
    rank_size = proj_input.shape[0]
    rev_pairs = rev_slot.shape[0] // 2
    example_at = lax.axis_index("example")
    tensor_at = lax.axis_index("tensor")
    near, far = example_at % 2, example_at // 2
    half_hidden = hidden_local // 2
    chunks = capacity // (2 * LANES)
    offset = (near * (half_hidden // TILE)).astype(jnp.int32).reshape(1)
    near_at, far_at = near.astype(jnp.int32).reshape(1), far.astype(jnp.int32).reshape(1)
    near_far = jnp.concatenate([near_at, far_at])
    gathered = [lax.all_gather(blocks[k], "tensor", axis=0, tiled=True) for k in range(2)]

    tile_count = half_hidden // TILE
    split = tile_count - tile_count // 2
    tile_parts = [(0, split), (split, tile_count - split)]

    def near_pair(rows, index):
        return rows, swap(rows, "example", 1), index

    def run(h, far, own, after):
        return stage(offset, near_far, tile_parts[h], far, own, down_weight, weight_near, after)

    weight_near = swap(down_weight, "example", 1)
    gate_rows = gate_pre.reshape(row_total, hidden_local)
    up_rows = up_pre.reshape(row_total, hidden_local)
    gate_near, up_near = swap(gate_rows, "example", 1), swap(up_rows, "example", 1)
    crossed = [move(blocks[k], CROSS) for k in range(2, chunks)]
    away = cut(1 - far_at, gathered[0], crossed)
    inputs_rows = layer_input.reshape(row_total, width_local)
    gate_values = gate_rows.astype(jnp.float32)
    up_values = up_rows.astype(jnp.float32)
    hidden = (gate_values * jax.nn.sigmoid(gate_values) * up_values).astype(jnp.bfloat16)
    early = jnp.concatenate(
        [
            contract(proj_input, inputs_rows),
            contract(proj_hidden, hidden),
            contract(proj_output, grad_rows),
        ]
    )
    def quarter(bits):
        return take(early, (tensor_at ^ bits) * slot_len, slot_len, 1)

    sums = [quarter(0)] + [swap(quarter(bits), "tensor", bits) for bits in (1, 2, 3)]
    far_pair = near_pair(swap(away, "example", 2), in_half)

    order = jnp.where(far == 1, 3 - tensor_at, tensor_at)
    shards = []
    for k in range(2, chunks):
        keep, send = pair_halves(blocks[k], crossed[k - 2], (away,))
        shards.append(jnp.where(order < 2, keep, move(send, SPREAD)))
    gathered += [lax.all_gather(shard, "tensor", axis=0, tiled=True) for shard in shards]

    came, right, after = [], [], ()
    for h, tiles in enumerate(tile_parts):
        if h == 1:
            after += tuple(shards)
        results = run(h, far_pair, None, after)
        came.append((swap(results[0], "example", 2), tiles[0]))
        after = (results[0],)
    before = near_pair(gathered[0], in_whole)
    for k in range(1, chunks):
        if k == 1:
            away = cut(1 - far_at, gathered[1], after)
            far_next = swap(away, "example", 2)
            after = (away, came[0][0])
            gate_packed = pack(chunks, 2 * LANES, half_hidden, offset, place, gate_rows, gate_near, after)
            up_packed = pack(chunks, 2 * LANES, half_hidden, offset, place, up_rows, up_near, after)
            after = (gate_packed[0], up_packed[0])
            far_pair = near_pair(ordered(far_next, after), in_half)
            own_pair = near_pair(gathered[1], in_whole)
        else:
            both = near_pair(gathered[k], None)[:2]
            far_pair = (*both, functools.partial(in_spread, 1))
            own_pair = (*both, functools.partial(in_spread, 0))
        arrived, came = came, []
        for h, tiles in enumerate(tile_parts):
            own = (*before, arrived[h], gate_packed[k - 1], up_packed[k - 1])
            results = run(h, far_pair, (*own, proj_gate, proj_up), after)
            after = (results[0],)
            came.append((swap(results[0], "example", 2), tiles[0]))
            right.append(results[1])
            if (k, h) == (1, 0):
                sums = sum_parts(sums, after)
                after += (sums,)
                in_gate, in_down, out_down = (sums[j * rank_size : (j + 1) * rank_size] for j in range(3))
                in_gate = [in_gate] + [swap(in_gate, "tensor", bits) for bits in (1, 2, 3)]
            if (k, h) == (1, 1):
                in_gate = join_parts(tensor_at.astype(jnp.int32).reshape(1), in_gate, (*after, came[0][0]))
                after += (in_gate,)
                in_gate_near = swap(in_gate, "example", 1)
        before = own_pair
    for h, tiles in enumerate(tile_parts):
        own = (*before, came[h], gate_packed[-1], up_packed[-1], proj_gate, proj_up)
        right += run(h, None, own, after)
        after = (right[-1],)
    right = jnp.concatenate([right[k] + right[k + 1] for k in range(0, 2 * chunks, 2)], axis=1)

    slots_here = jnp.concatenate(
        [
            take(rev_slot, example_at * ex_count, ex_count, 0),
            take(rev_slot, (example_at ^ 1) * ex_count, ex_count, 0),
        ]
    )
    table = pairing_table(slots_here, rev_pairs)
    positions = jnp.arange(slot_len, dtype=jnp.int32)
    mask = (positions < take(own_lengths, tensor_at, 1, 0)).astype(jnp.float32)
    sketch_down = contract_exact(in_down * mask[None, :], out_down)
    sketch_down = take(table, tensor_at, 1, 1)[:, :, None] * sketch_down[None, :, :]
    select = jnp.arange(capacity, dtype=jnp.int32)[:, None] == place
    in_gate = jnp.concatenate([in_gate, in_gate_near], axis=1)
    in_gate = contract_exact(in_gate, select.astype(jnp.float32))
    table_rows = contract(
        jnp.repeat(table, slot_len, axis=1).astype(jnp.bfloat16), select.astype(jnp.bfloat16)
    )
    left = (table_rows[:, None, :] * in_gate[None, :, :]).reshape(rev_pairs * rank_size, capacity)
    sketch_late = contract_exact(left, right).reshape(rev_pairs, rank_size, 2 * rank_size)
    return jnp.concatenate([sketch_late, sketch_down], axis=2)


def local_four(
    layer_input,
    gate_pre,
    up_pre,
    output_grad,
    down_weight,
    proj_input,
    proj_hidden,
    proj_output,
    proj_gate,
    proj_up,
    query_sketches,
    rev_lengths,
    rev_slot,
    query_slot,
):
    ex_count, slot_len, width_local = layer_input.shape
    row_total = ex_count * slot_len
    grad_rows = output_grad.reshape(row_total, width_local)
    grad_near = swap(grad_rows, "example", 1)
    others = [swap(rev_lengths, "example", bits) for bits in (1, 2, 3)]

    near = lax.axis_index("example") % 2
    both_lengths = jnp.concatenate([rev_lengths, others[0]])
    own_begin = near * jnp.sum(others[0])
    near_begin = (1 - near) * jnp.sum(rev_lengths)
    offsets = jnp.concatenate(
        [
            own_begin + jnp.cumsum(rev_lengths) - rev_lengths,
            near_begin + jnp.cumsum(others[0]) - others[0],
        ]
    )
    positions = jnp.arange(slot_len, dtype=jnp.int32)
    place = (offsets[:, None] + positions[None, :]) ^ (near * LANES)
    place = jnp.where(positions[None, :] < both_lengths[:, None], place, -1).reshape(1, 2 * row_total)
    no_offset = jnp.zeros((1,), jnp.int32)
    full = 2 * row_total
    blocks = pack(full // (2 * LANES), LANES, width_local, no_offset, place, grad_rows, grad_near)
    sums = jnp.stack([jnp.sum(rev_lengths) + jnp.sum(others[0]), jnp.sum(others[1]) + jnp.sum(others[2])])
    most = jnp.max(sums).reshape(1)
    count = lax.axis_size("group")
    for step in range(1, count):
        shifted = lax.ppermute(most, "group", [(i, (i + step) % count) for i in range(count)])
        most = jnp.maximum(most, shifted)
    levels = [level for level in LEVELS if level < full] + [full]
    branch = jnp.sum((most[0] > jnp.array(levels[:-1], jnp.int32)).astype(jnp.int32))
    sketch = lax.switch(
        branch,
        [functools.partial(packed_scores, level) for level in levels],
        (
            layer_input,
            gate_pre,
            up_pre,
            grad_rows,
            blocks,
            place,
            down_weight,
            proj_input,
            proj_hidden,
            proj_output,
            proj_gate,
            proj_up,
            rev_slot,
            rev_lengths,
        ),
    )
    rank_size = proj_input.shape[0]
    rev_pairs = rev_slot.shape[0] // 2
    revision_pairs = sum_over(scatter_over(sketch, "tensor", 1), "example")
    example_scores = contract_exact(
        revision_pairs.reshape(rev_pairs, -1), query_sketches.astype(jnp.float32)
    )
    query_pairs = query_slot.shape[0] * 4 // 2
    pair_terms = contract_exact(example_scores, pairing_table(query_slot, query_pairs))
    total = sum_over(scatter_over(pair_terms, "example", 1), "tensor")
    return total / jnp.float32(rank_size * rank_size)


def local_any(
    layer_input,
    gate_pre,
    up_pre,
    output_grad,
    down_weight,
    proj_input,
    proj_hidden,
    proj_output,
    proj_gate,
    proj_up,
    query_sketches,
    rev_lengths,
    rev_slot,
    query_slot,
):
    ex_count, slot_len, width_local = layer_input.shape
    hidden_local = gate_pre.shape[2]
    row_total = ex_count * slot_len
    rank_size = proj_input.shape[0]
    per_rank = rank_size // lax.axis_size("tensor")
    inputs_rows = layer_input.reshape(row_total, width_local)
    grad_rows = output_grad.reshape(row_total, width_local)
    gate_values = gate_pre.reshape(row_total, hidden_local).astype(jnp.float32)
    up_values = up_pre.reshape(row_total, hidden_local).astype(jnp.float32)
    grad_full = lax.all_gather(grad_rows, "tensor", axis=1, tiled=True)
    hidden_grad = contract(grad_full, lax.all_gather(down_weight, "example", axis=1, tiled=True))
    hidden_grad = lax.optimization_barrier(hidden_grad.astype(jnp.bfloat16)).astype(jnp.float32)
    sigma = jax.nn.sigmoid(gate_values)
    active = gate_values * sigma
    hidden = (active * up_values).astype(jnp.bfloat16)
    grad_up = (hidden_grad * active).astype(jnp.bfloat16)
    grad_gate = (hidden_grad * up_values * sigma * (1.0 + gate_values * (1.0 - sigma))).astype(
        jnp.bfloat16
    )
    partials = jnp.stack(
        [
            contract(inputs_rows, proj_input),
            contract(hidden, proj_hidden),
            contract(grad_gate, proj_gate),
            contract(grad_up, proj_up),
            contract(grad_rows, proj_output),
        ]
    )
    summed = lax.psum(partials, "tensor")
    begin = lax.axis_index("tensor") * per_rank
    left = lax.dynamic_slice_in_dim(summed[:2], begin, per_rank, 2)
    right = summed[2:]
    positions = jnp.arange(slot_len, dtype=jnp.int32)
    mask = (positions[None, :] < rev_lengths[:, None]).astype(jnp.float32).reshape(row_total)
    left = left * mask[None, :, None]
    left = jnp.stack([left[0], left[0], left[1]]).reshape(3, ex_count, slot_len, per_rank)
    right = right.reshape(3, ex_count, slot_len, rank_size)
    sketches = jnp.einsum("meti,metj->eimj", left, right, precision=lax.Precision.HIGHEST).reshape(
        ex_count, per_rank * 3 * rank_size
    )
    every_sketch = lax.all_gather(sketches, "example", axis=0, tiled=True)
    rev_pairs = rev_slot.shape[0] // 2
    revision_pairs = jnp.dot(
        pairing_table(rev_slot, rev_pairs), every_sketch, precision=lax.Precision.HIGHEST
    )
    example_scores = contract_exact(revision_pairs, query_sketches.astype(jnp.float32))
    query_pairs = query_slot.shape[0] * lax.axis_size("example") // 2
    pair_terms = contract_exact(example_scores, pairing_table(query_slot, query_pairs))
    owned = lax.psum_scatter(pair_terms, "example", scatter_dimension=1, tiled=True)
    total = lax.psum(owned, "tensor")
    return total / jnp.float32(rank_size * rank_size)


def solution(mesh):
    four = mesh.shape["tensor"] == 4 and mesh.shape["example"] == 4
    return jax.shard_map(
        local_four if four else local_any,
        mesh=mesh,
        in_specs=(
            P(("group", "example"), None, "tensor"),
            P(("group", "example"), None, "tensor"),
            P(("group", "example"), None, "tensor"),
            P(("group", "example"), None, "tensor"),
            P("tensor", "example"),
            P(None, "tensor"),
            P(None, "tensor"),
            P(None, "tensor"),
            P(None, "tensor"),
            P(None, "tensor"),
            P(("group", "example"), "tensor"),
            P(("group", "example")),
            P("group"),
            P(("group", "example")),
        ),
        out_specs=P("group", "example"),
        check_vma=False,
    )
```

profile of v0, /device:TPU:0, one launch (start us, length us, event | category | flops | bytes accessed | tf_op | source)
XLA Modules:
  0.0 395.6 jit_solution(5012066818314868100)
XLA Ops:
  7.0 2.9 collective-permute-start.56
  12.2 1.3 bitcast_subtract_fusion.1
  17.8 3.9 collective-permute-start.58
  23.2 6.0 %pack_rows.9 = (bf16[2048,128]{1,0:T(8,128)(2,1)}, bf16[2048,128]{1,0:T(8,128)(2,1)}, bf16[2048,128]{1,0:T(8,128)(2,1)}, bf16[2048,128]{1,0:T(8,128)(2,1)}) custom-call(s32[1]{0:T(128)} %constant.189.clone.1.near_ref, s32[1,1024]{1,0:T(1,128)S(1)} %bitcast.71, bf16[512,2048]{1,0:T(8,128)(2,1)} %bitcast.68, bf16[512,2048]{1,0:T(8,128)(2,1)} %collective-permute-done.59.other_ref), custom_call_target="tpu_custom_call" | custom-call | flops 2147483648 | bytes 6291456 | tf_op jit(solution)/shard_map/pack_rows/pallas_call | solution.py:94
  29.3 322.9 %conditional.1 = (f32[8,64,192]{2,1,0:T(8,128)S(1)}) conditional(s32[]{:T(128)} %bitcast.25, (s32[16]{0:T(128)S(1)}, s32[1,1024]{1,0:T(1,128)S(1)}, bf16[4,128,2048]{2,1,0:T(8,128)(2,1)}, bf16[64,2048]{1,0:T(8,128)(2,1)}, bf16[4,128,7168]{2,1,0:T(8,128)(2,1)}, /*index=5*/bf16[4,128,7168]{2,1,0:T(8,128)(2,1)}, bf16[64,7168]{1,0:T(8,128)(2,1)}, ...), branch_computations={%region_6.7_spmd, %region_7.8_spmd} | conditional | flops 77567238144 | bytes 580137728 | solution.py:538
  30.6 1.3 collective-permute-start.4
  31.9 14.8 %collective-permute-done.4.refs_0_.b = bf16[2048,128]{1,0:T(8,128)(2,1)} collective-permute-done((bf16[2048,128]{1,0:T(8,128)(2,1)}, bf16[2048,128]{1,0:T(8,128)(2,1)}, u32[]{:S(2)}, u32[]{:S(2)}) %collective-permute-start.4) | collective-permute-done | bytes 524320 | tf_op jit(solution)/shard_map/cond/branch_0_fun/ppermute | solution.py:65
  46.8 32.1 %all-gather.10.cloned.1.call-done.source.refs_12_.refs_14_.refs_16_.refs_18_ = bf16[8192,128]{1,0:T(8,128)(2,1)} async-done(((bf16[2048,128]{1,0:T(8,128)(2,1)}), bf16[8192,128]{1,0:T(8,128)(2,1)}) %all-gather.10.cloned.1.call-update) | async-done | bytes 2097168 | tf_op jit(solution)/shard_map/cond/branch_0_fun/all_gather | solution.py:383
  78.8 3.4 cut_columns.4.refs_0_
  82.2 1.5 collective-permute-start.5
  83.8 2.3 pair_halves.3
  86.1 3.9 collective-permute-start.7
  90.0 17.5 %collective-permute-done.5.refs_4_.refs_6_.refs_8_.refs_10_ = bf16[4096,128]{1,0:T(8,128)(2,1)} collective-permute-done((bf16[4096,128]{1,0:T(8,128)(2,1)}, bf16[4096,128]{1,0:T(8,128)(2,1)}, u32[]{:S(2)}, u32[]{:S(2)}) %collective-permute-start.5) | collective-permute-done | bytes 1048608 | tf_op jit(solution)/shard_map/cond/branch_0_fun/ppermute | solution.py:46
  107.4 8.5 %fusion.13 = f32[64,512]{1,0:T(8,128)} fusion(bf16[64,7168]{1,0:T(8,128)(2,1)S(1)} %copy-done.59, bf16[512,7168]{1,0:T(8,128)(2,1)} %bitcast.87, bf16[512,7168]{1,0:T(8,128)(2,1)} %bitcast.81), kind=kOutput, calls=%fused_computation.15 | convolution fusion | flops 499122176 | bytes 15728640 | tf_op jit(solution)/shard_map/cond/branch_0_fun/dot_general | solution.py:18
  116.6 2.4 fusion.89
  120.0 11.8 %stage.18.refs_12_ = bf16[2048,256]{1,0:T(8,128)(2,1)} custom-call(s32[1]{0:T(128)} %bitcast.6.offset_ref.near_ref, s32[2]{0:T(128)} %pad_add_fusion.1.near_ref, bf16[7168,2048]{1,0:T(8,128)(2,1)} %get-tuple-element.83.refs_0_.refs_1_, bf16[7168,2048]{1,0:T(8,128)(2,1)} %get-tuple-element.83.refs_0_.refs_1_, ...), custom_call_target="tpu_custom_call" | custom-call | flops 4294967296 | bytes 18874368 | tf_op jit(solution)/shard_map/cond/branch_0_fun/stage/pallas_call | solution.py:321
  131.8 23.8 %collective-permute-start.10 = (bf16[2048,256]{1,0:T(8,128)(2,1)}, bf16[2048,256]{1,0:T(8,128)(2,1)}, u32[]{:S(2)}, u32[]{:S(2)}) collective-permute-start(bf16[2048,256]{1,0:T(8,128)(2,1)} %stage.18.refs_12_), channel_id=1, source_target_pairs={{0,2},{1,3},{2,0},{3,1},{4,6},{5,7},{6,4},{7,5},{8,10},{9,11},{10,... | collective-permute-start | bytes 3145736 | tf_op jit(solution)/shard_map/cond/branch_0_fun/ppermute | solution.py:46
  157.4 10.0 %stage.19.refs_0_ = bf16[1536,256]{1,0:T(8,128)(2,1)} custom-call(s32[1]{0:T(128)} %bitcast.6.offset_ref.near_ref, s32[2]{0:T(128)} %pad_add_fusion.1.near_ref, bf16[7168,2048]{1,0:T(8,128)(2,1)} %get-tuple-element.83.refs_0_.refs_1_, bf16[7168,2048]{1,0:T(8,128)(2,1)} %get-tuple-element.83.refs_0_.refs_1_, ...), custom_call_target="tpu_custom_call" | custom-call | flops 3221225472 | bytes 14155776 | tf_op jit(solution)/shard_map/cond/branch_0_fun/stage/pallas_call | solution.py:321
  167.4 3.4 cut_columns.5.refs_0_
  170.8 9.1 %collective-permute-done.10.refs_1_.refs_20_ = bf16[2048,256]{1,0:T(8,128)(2,1)} collective-permute-done((bf16[2048,256]{1,0:T(8,128)(2,1)}, bf16[2048,256]{1,0:T(8,128)(2,1)}, u32[]{:S(2)}, u32[]{:S(2)}) %collective-permute-start.10) | collective-permute-done | bytes 1048608 | tf_op jit(solution)/shard_map/cond/branch_0_fun/ppermute | solution.py:46
  179.9 10.4 %pack_rows.6 = (bf16[3584,256]{1,0:T(8,128)(2,1)}, bf16[3584,256]{1,0:T(8,128)(2,1)}, bf16[3584,256]{1,0:T(8,128)(2,1)}) custom-call(s32[1]{0:T(128)} %bitcast.6.offset_ref.near_ref, s32[1,1024]{1,0:T(1,128)S(1)} %get-tuple-element.75.place_ref, bf16[512,7168]{1,0:T(8,128)(2,1)} %bitcast.88, bf16[512,7168]{1,0:T(8,128)(2,1)} %collective-permute-done.11.other_ref, ...), custom_call_target="tpu_custom_call" | custom-call | flops 5637144576 | bytes 12845056 | tf_op jit(solution)/shard_map/cond/branch_0_fun/pack_rows/pallas_call | solution.py:94
  190.4 10.4 %pack_rows.5 = (bf16[3584,256]{1,0:T(8,128)(2,1)}, bf16[3584,256]{1,0:T(8,128)(2,1)}, bf16[3584,256]{1,0:T(8,128)(2,1)}) custom-call(s32[1]{0:T(128)} %bitcast.6.offset_ref.near_ref, s32[1,1024]{1,0:T(1,128)S(1)} %get-tuple-element.75.place_ref, bf16[512,7168]{1,0:T(8,128)(2,1)} %bitcast.82, bf16[512,7168]{1,0:T(8,128)(2,1)} %collective-permute-done.9.other_ref, ...), custom_call_target="tpu_custom_call" | custom-call | flops 5637144576 | bytes 12845056 | tf_op jit(solution)/shard_map/cond/branch_0_fun/pack_rows/pallas_call | solution.py:94
  201.5 1.0 copy-done.15
  202.4 2.3 ordered_copy.2.refs_4_.refs_6_.refs_8_.refs_10_
  206.3 1.2 fusion.8
  207.7 1.7 collective-permute-start.17
  209.4 18.3 %stage.20 = (bf16[2048,256]{1,0:T(8,128)(2,1)}, f32[128,256]{1,0:T(8,128)}) custom-call(s32[1]{0:T(128)} %bitcast.6.offset_ref.near_ref, s32[2]{0:T(128)} %pad_add_fusion.1.near_ref, bf16[7168,2048]{1,0:T(8,128)(2,1)} %get-tuple-element.83.refs_0_.refs_1_, bf16[7168,2048]{1,0:T(8,128)(2,1)} %get-tuple-element.83.refs_0_.refs_1_, ...), custom_call_target="tpu_custom_call" | custom-call | flops 8589934592 | bytes 20971520 | tf_op jit(solution)/shard_map/cond/branch_0_fun/stage/pallas_call | solution.py:321
  228.8 3.1 collective-permute-start.2
  231.9 3.4 collective-permute-done.2.d
  236.0 1.7 sum_parts.2.refs_26_
  238.4 2.6 collective-permute-start.14
  241.0 1.1 collective-permute-start.15
  242.1 15.4 %stage.21 = (bf16[1536,256]{1,0:T(8,128)(2,1)}, f32[128,256]{1,0:T(8,128)}) custom-call(s32[1]{0:T(128)} %bitcast.6.offset_ref.near_ref, s32[2]{0:T(128)} %pad_add_fusion.1.near_ref, bf16[7168,2048]{1,0:T(8,128)(2,1)} %get-tuple-element.83.refs_0_.refs_1_, bf16[7168,2048]{1,0:T(8,128)(2,1)} %get-tuple-element.83.refs_0_.refs_1_, ...), custom_call_target="tpu_custom_call" | custom-call | flops 6442450944 | bytes 15728640 | tf_op jit(solution)/shard_map/cond/branch_0_fun/stage/pallas_call | solution.py:321
  257.5 1.9 collective-permute-start.16
  259.6 1.6 add.173
  261.2 1.3 collective-permute-start.22
  264.3 1.5 join_parts.2.refs_26_
  265.8 18.3 %stage.22 = (bf16[2048,256]{1,0:T(8,128)(2,1)}, f32[128,256]{1,0:T(8,128)}) custom-call(s32[1]{0:T(128)} %bitcast.6.offset_ref.near_ref, s32[2]{0:T(128)} %pad_add_fusion.1.near_ref, bf16[7168,2048]{1,0:T(8,128)(2,1)} %get-tuple-element.83.refs_0_.refs_1_, bf16[7168,2048]{1,0:T(8,128)(2,1)} %get-tuple-element.83.refs_0_.refs_1_, ...), custom_call_target="tpu_custom_call" | custom-call | flops 8589934592 | bytes 20971520 | tf_op jit(solution)/shard_map/cond/branch_0_fun/stage/pallas_call | solution.py:321
  284.1 1.0 collective-permute-start.23
  286.1 15.1 %stage.23 = (bf16[1536,256]{1,0:T(8,128)(2,1)}, f32[128,256]{1,0:T(8,128)}) custom-call(s32[1]{0:T(128)} %bitcast.6.offset_ref.near_ref, s32[2]{0:T(128)} %pad_add_fusion.1.near_ref, bf16[7168,2048]{1,0:T(8,128)(2,1)} %get-tuple-element.83.refs_0_.refs_1_, bf16[7168,2048]{1,0:T(8,128)(2,1)} %get-tuple-element.83.refs_0_.refs_1_, ...), custom_call_target="tpu_custom_call" | custom-call | flops 6442450944 | bytes 15728640 | tf_op jit(solution)/shard_map/cond/branch_0_fun/stage/pallas_call | solution.py:321
  301.2 1.1 collective-permute-start.24
  302.4 0.9 add.174
  303.4 2.4 fusion.7
  305.8 4.6 %collective-permute-done.23.refs_12_ = bf16[2048,256]{1,0:T(8,128)(2,1)S(1)} collective-permute-done((bf16[2048,256]{1,0:T(8,128)(2,1)}, bf16[2048,256]{1,0:T(8,128)(2,1)S(1)}, u32[]{:S(2)}, u32[]{:S(2)}) %collective-permute-start.23) | collective-permute-done | bytes 1048608 | tf_op jit(solution)/shard_map/cond/branch_0_fun/ppermute | solution.py:46
  310.4 1.0 copy-done.11
  311.3 13.3 %stage.24.refs_17_ = f32[128,256]{1,0:T(8,128)} custom-call(s32[1]{0:T(128)} %bitcast.6.offset_ref.near_ref, s32[2]{0:T(128)} %pad_add_fusion.1.near_ref, bf16[7168,2048]{1,0:T(8,128)(2,1)} %get-tuple-element.83.refs_0_.refs_1_, bf16[7168,2048]{1,0:T(8,128)(2,1)} %get-tuple-element.83.refs_0_.refs_1_, ...), custom_call_target="tpu_custom_call" | custom-call | flops 4294967296 | bytes 18874368 | tf_op jit(solution)/shard_map/cond/branch_0_fun/stage/pallas_call | solution.py:321
  324.7 2.1 collective-permute-done.24.refs_12_
  327.7 11.2 %stage.25 = f32[128,256]{1,0:T(8,128)} custom-call(s32[1]{0:T(128)} %bitcast.6.offset_ref.near_ref, s32[2]{0:T(128)} %pad_add_fusion.1.near_ref, bf16[7168,2048]{1,0:T(8,128)(2,1)} %get-tuple-element.83.refs_0_.refs_1_, bf16[7168,2048]{1,0:T(8,128)(2,1)} %get-tuple-element.83.refs_0_.refs_1_, bf16[7168,2048]{1,0:T(8,128)(2,1)} %collective-permute-done.3.refs_2_.refs_3_, ...), custom_call_target="tpu_custom_call" | custom-call | flops 3221225472 | bytes 14155776 | tf_op jit(solution)/shard_map/cond/branch_0_fun/stage/pallas_call | solution.py:321
  338.9 0.9 add.175
  339.8 1.4 fusion.9
  352.2 2.4 collective-permute-start.61
  354.6 2.0 collective-permute-start.62
  356.6 2.4 collective-permute-done.60
  359.0 6.1 %collective-permute-done.61 = f32[8,16,192]{2,1,0:T(8,128)S(1)} collective-permute-done((f32[8,16,192]{2,1,0:T(8,128)S(1)}, f32[8,16,192]{2,1,0:T(8,128)S(1)}, u32[]{:S(2)}, u32[]{:S(2)}) %collective-permute-start.61) | collective-permute-done | bytes 98336 | tf_op jit(solution)/shard_map/ppermute | solution.py:46
  365.3 1.1 collective-permute-start.64
  367.2 4.5 %collective-permute-done.64 = f32[8,16,192]{2,1,0:T(8,128)S(1)} collective-permute-done((f32[8,16,192]{2,1,0:T(8,128)S(1)}, f32[8,16,192]{2,1,0:T(8,128)S(1)}, u32[]{:S(2)}, u32[]{:S(2)}) %collective-permute-start.64) | collective-permute-done | bytes 98336 | tf_op jit(solution)/shard_map/ppermute | solution.py:46
  371.6 1.9 collective-permute-done.65
  373.7 1.3 fusion.93
  375.9 1.0 collective-permute-start.67
  377.4 2.0 collective-permute-done.67
  379.9 2.1 collective-permute-start.69
  382.8 1.7 collective-permute-start.71
  384.5 2.1 collective-permute-done.70
  386.5 1.7 collective-permute-done.71
  (160 shorter events, 22.5 us)
Async XLA Ops:
  6.5 367.1 %copy-start = (bf16[256,3072]{1,0:T(8,128)(2,1)S(1)}, bf16[256,3072]{1,0:T(8,128)(2,1)}, u32[]{:S(2)}) copy-start(bf16[256,3072]{1,0:T(8,128)(2,1)} %param.27) | copy-start | bytes 4718596
  6.5 16.6 %collective-permute-start.59 = (bf16[512,2048]{1,0:T(8,128)(2,1)}, bf16[512,2048]{1,0:T(8,128)(2,1)}, u32[]{:S(2)}, u32[]{:S(2)}) collective-permute-start(bf16[512,2048]{1,0:T(8,128)(2,1)} %bitcast.67), channel_id=1, source_target_pairs={{0,1},{1,0},{2,3},{3,2},{4,5},{5,4},{6,7},{7,6},{8,9},{9,8},{10,11... | collective-permute-start | bytes 6291464 | tf_op jit(solution)/shard_map/ppermute | solution.py:46
  7.0 3.9 collective-permute-start.55
  7.0 8.3 %collective-permute-start.56 = (s32[4]{0:T(128)}, s32[4]{0:T(128)S(1)}, u32[]{:S(2)}, u32[]{:S(2)}) collective-permute-start(s32[4]{0:T(128)} %param.28), channel_id=1, source_target_pairs={{0,2},{1,3},{2,0},{3,1},{4,6},{5,7},{6,4},{7,5},{8,10},{9,11},{10,... | collective-permute-start | bytes 56 | tf_op jit(solution)/shard_map/ppermute | solution.py:46
  10.0 6.0 %collective-permute-start.57 = (s32[4]{0:T(128)}, s32[4]{0:T(128)S(1)}, u32[]{:S(2)}, u32[]{:S(2)}) collective-permute-start(s32[4]{0:T(128)} %param.28), channel_id=1, source_target_pairs={{0,3},{1,2},{2,1},{3,0},{4,7},{5,6},{6,5},{7,4},{8,11},{9,10},{10,... | collective-permute-start | bytes 56 | tf_op jit(solution)/shard_map/ppermute | solution.py:46
  17.8 4.8 %collective-permute-start.58 = (s32[1]{0:T(128)}, s32[1]{0:T(128)}, u32[]{:S(2)}, u32[]{:S(2)}) collective-permute-start(s32[1]{0:T(128)} %bitcast.24), channel_id=1, source_target_pairs={{0,16},{16,0},{1,17},{17,1},{2,18},{18,2},{3,19},{19,3},{4,20},{20... | collective-permute-start | bytes 20 | tf_op jit(solution)/shard_map/ppermute | solution.py:534
  23.2 6.0 %copy-start.2 = (bf16[64,7168]{1,0:T(8,128)(2,1)S(1)}, bf16[64,7168]{1,0:T(8,128)(2,1)}, u32[]{:S(2)}) copy-start(bf16[64,7168]{1,0:T(8,128)(2,1)} %param.25) | copy-start | bytes 2752516
  29.2 337.9 %copy-start.54 = (s32[256]{0:T(256)S(1)}, s32[256]{0:T(256)}, u32[]{:S(2)}) copy-start(s32[256]{0:T(256)} %param.30) | copy-start | bytes 3076
  29.3 177.0 %copy-start.52 = (s32[1,1024]{1,0:T(1,128)}, s32[1,1024]{1,0:T(1,128)S(1)}, u32[]{:S(2)}) copy-start(s32[1,1024]{1,0:T(1,128)S(1)} %get-tuple-element.75.place_ref) | copy-start | bytes 12292 | tf_op jit(solution)/shard_map/cond
  29.3 49.6 %all-gather.10.cloned.1.call-start = ((), (), s32[]{:S(2)}) async-start(), calls=%async_computation.1 | async-start | bytes 2621440 | tf_op jit(solution)/shard_map/cond/branch_0_fun/all_gather | solution.py:383
  29.3 90.6 %collective-permute-start.3 = (bf16[7168,2048]{1,0:T(8,128)(2,1)}, bf16[7168,2048]{1,0:T(8,128)(2,1)}, u32[]{:S(2)}, u32[]{:S(2)}) collective-permute-start(bf16[7168,2048]{1,0:T(8,128)(2,1)} %get-tuple-element.83.refs_0_.refs_1_), channel_id=1, source_target_pairs={{0,1},{1,0},{2,3},{3,2},{4,5},{5,4},{6,7},{7,6},{8,9},{9,8},{10,11... | collective-permute-start | bytes 88080392 | tf_op jit(solution)/shard_map/cond/branch_0_fun/ppermute | solution.py:46
  30.0 137.4 %all-gather.8.cloned.1.call-start = ((), (), s32[]{:S(2)}) async-start(), calls=%async_computation | async-start | bytes 2621440 | tf_op jit(solution)/shard_map/cond/branch_0_fun/all_gather | solution.py:383
  30.1 140.7 %collective-permute-start.11 = (bf16[512,7168]{1,0:T(8,128)(2,1)}, bf16[512,7168]{1,0:T(8,128)(2,1)}, u32[]{:S(2)}, u32[]{:S(2)}) collective-permute-start(bf16[512,7168]{1,0:T(8,128)(2,1)} %bitcast.86), channel_id=1, source_target_pairs={{0,1},{1,0},{2,3},{3,2},{4,5},{5,4},{6,7},{7,6},{8,9},{9,8},{10,11... | collective-permute-start | bytes 22020104 | tf_op jit(solution)/shard_map/cond/branch_0_fun/ppermute | solution.py:46
  30.1 160.2 %collective-permute-start.9 = (bf16[512,7168]{1,0:T(8,128)(2,1)}, bf16[512,7168]{1,0:T(8,128)(2,1)}, u32[]{:S(2)}, u32[]{:S(2)}) collective-permute-start(bf16[512,7168]{1,0:T(8,128)(2,1)} %bitcast.80), channel_id=1, source_target_pairs={{0,1},{1,0},{2,3},{3,2},{4,5},{5,4},{6,7},{7,6},{8,9},{9,8},{10,11... | collective-permute-start | bytes 22020104 | tf_op jit(solution)/shard_map/cond/branch_0_fun/ppermute | solution.py:46
  30.6 16.1 %collective-permute-start.4 = (bf16[2048,128]{1,0:T(8,128)(2,1)}, bf16[2048,128]{1,0:T(8,128)(2,1)}, u32[]{:S(2)}, u32[]{:S(2)}) collective-permute-start(bf16[2048,128]{1,0:T(8,128)(2,1)} %get-tuple-element.86.a), channel_id=1, source_target_pairs={{2,0},{3,1},{6,4},{7,5},{8,10},{9,11},{12,14},{13,15},{18,16},{19,... | collective-permute-start | bytes 1572872 | tf_op jit(solution)/shard_map/cond/branch_0_fun/ppermute | solution.py:65
  82.2 25.2 %collective-permute-start.5 = (bf16[4096,128]{1,0:T(8,128)(2,1)}, bf16[4096,128]{1,0:T(8,128)(2,1)}, u32[]{:S(2)}, u32[]{:S(2)}) collective-permute-start(bf16[4096,128]{1,0:T(8,128)(2,1)} %cut_columns.4.refs_0_), channel_id=1, source_target_pairs={{0,2},{1,3},{2,0},{3,1},{4,6},{5,7},{6,4},{7,5},{8,10},{9,11},{10,... | collective-permute-start | bytes 3145736 | tf_op jit(solution)/shard_map/cond/branch_0_fun/ppermute | solution.py:46
  83.7 121.7 %all-gather.12.cloned.1.call-start = ((), (), s32[]{:S(2)}) async-start(), calls=%async_computation.2 | async-start | bytes 2621440 | tf_op jit(solution)/shard_map/cond/branch_0_fun/all_gather | solution.py:423
  83.8 23.7 %copy-start.59 = (bf16[64,7168]{1,0:T(8,128)(2,1)S(1)}, bf16[64,7168]{1,0:T(8,128)(2,1)}, u32[]{:S(2)}) copy-start(bf16[64,7168]{1,0:T(8,128)(2,1)} %get-tuple-element.80) | copy-start | bytes 2752516 | tf_op jit(solution)/shard_map/cond
  86.1 32.9 %collective-permute-start.7 = (bf16[2048,128]{1,0:T(8,128)(2,1)}, bf16[2048,128]{1,0:T(8,128)(2,1)}, u32[]{:S(2)}, u32[]{:S(2)}) collective-permute-start(bf16[2048,128]{1,0:T(8,128)(2,1)} %get-tuple-element.88), channel_id=1, source_target_pairs={{0,8},{1,9},{4,12},{5,13},{10,2},{11,3},{14,6},{15,7},{16,24},{17,... | collective-permute-start | bytes 1572872 | tf_op jit(solution)/shard_map/cond/branch_0_fun/ppermute | solution.py:65
  107.4 12.5 %collective-permute-start.6 = (bf16[4096,128]{1,0:T(8,128)(2,1)}, bf16[4096,128]{1,0:T(8,128)(2,1)}, u32[]{:S(2)}, u32[]{:S(2)}) collective-permute-start(bf16[4096,128]{1,0:T(8,128)(2,1)} %collective-permute-done.5.refs_4_.refs_6_.refs_8_.refs_10_), channel_id=1, source_target_pairs={{0,1},{1,0},{2,3},{3,2},{4,5},{5,4},{6,7},{7,6},{8,9},{9,8},{10,11... | collective-permute-start | bytes 3145736 | tf_op jit(solution)/shard_map/cond/branch_0_fun/ppermute | solution.py:46
  120.0 35.7 %copy-start.4 = (bf16[512,2048]{1,0:T(8,128)(2,1)S(1)}, bf16[512,2048]{1,0:T(8,128)(2,1)}, u32[]{:S(2)}) copy-start(bf16[512,2048]{1,0:T(8,128)(2,1)} %get-tuple-element.82) | copy-start | bytes 6291460 | tf_op jit(solution)/shard_map/cond
  120.0 35.6 %copy-start.12 = (bf16[64,2048]{1,0:T(8,128)(2,1)S(1)}, bf16[64,2048]{1,0:T(8,128)(2,1)}, u32[]{:S(2)}) copy-start(bf16[64,2048]{1,0:T(8,128)(2,1)} %get-tuple-element.81) | copy-start | bytes 786436 | tf_op jit(solution)/shard_map/cond
  131.8 24.6 %copy-start.41 = (f32[64,512]{1,0:T(8,128)S(1)}, f32[64,512]{1,0:T(8,128)}, u32[]{:S(2)}) copy-start(f32[64,512]{1,0:T(8,128)} %fusion.13) | copy-start | bytes 393220 | tf_op jit(solution)/shard_map/cond
  131.8 48.1 %collective-permute-start.10 = (bf16[2048,256]{1,0:T(8,128)(2,1)}, bf16[2048,256]{1,0:T(8,128)(2,1)}, u32[]{:S(2)}, u32[]{:S(2)}) collective-permute-start(bf16[2048,256]{1,0:T(8,128)(2,1)} %stage.18.refs_12_), channel_id=1, source_target_pairs={{0,2},{1,3},{2,0},{3,1},{4,6},{5,7},{6,4},{7,5},{8,10},{9,11},{10,... | collective-permute-start | bytes 3145736 | tf_op jit(solution)/shard_map/cond/branch_0_fun/ppermute | solution.py:46
  157.2 70.5 %collective-permute-start = (f32[192,128]{1,0:T(8,128)}, f32[192,128]{1,0:T(8,128)}, u32[]{:S(2)}, u32[]{:S(2)}) collective-permute-start(f32[192,128]{1,0:T(8,128)} %get-tuple-element.161), channel_id=1, source_target_pairs={{0,4},{4,0},{8,12},{12,8},{1,5},{5,1},{9,13},{13,9},{2,6},{6,2},{1... | collective-permute-start | bytes 294920 | tf_op jit(solution)/shard_map/cond/branch_0_fun/ppermute | solution.py:46
  157.4 50.2 %collective-permute-start.13 = (bf16[8192,128]{1,0:T(8,128)(2,1)}, bf16[8192,128]{1,0:T(8,128)(2,1)}, u32[]{:S(2)}, u32[]{:S(2)}) collective-permute-start(bf16[8192,128]{1,0:T(8,128)(2,1)} %all-gather.10.cloned.1.call-done.source.refs_12_.refs_14_.refs_16_.refs_18_), channel_id=1, source_target_pairs={{0,1},{1,0},{2,3},{3,2},{4,5},{5,4},{6,7},{7,6},{8,9},{9,8},{10,11... | collective-permute-start | bytes 6291464 | tf_op jit(solution)/shard_map/cond/branch_0_fun/ppermute | solution.py:46
  170.7 30.7 %collective-permute-start.8 = (bf16[4096,128]{1,0:T(8,128)(2,1)}, bf16[4096,128]{1,0:T(8,128)(2,1)S(1)}, u32[]{:S(2)}, u32[]{:S(2)}) collective-permute-start(bf16[4096,128]{1,0:T(8,128)(2,1)} %cut_columns.5.refs_0_), channel_id=1, source_target_pairs={{0,2},{1,3},{2,0},{3,1},{4,6},{5,7},{6,4},{7,5},{8,10},{9,11},{10,... | collective-permute-start | bytes 3145736 | tf_op jit(solution)/shard_map/cond/branch_0_fun/ppermute | solution.py:46
  204.7 3.0 collective-permute-start.12
  204.9 60.9 %collective-permute-start.21 = (bf16[8192,128]{1,0:T(8,128)(2,1)}, bf16[8192,128]{1,0:T(8,128)(2,1)}, u32[]{:S(2)}, u32[]{:S(2)}) collective-permute-start(bf16[8192,128]{1,0:T(8,128)(2,1)} %all-gather.8.cloned.1.call-done.source.refs_12_.refs_14_.refs_16_.refs_18_), channel_id=1, source_target_pairs={{0,1},{1,0},{2,3},{3,2},{4,5},{5,4},{6,7},{7,6},{8,9},{9,8},{10,11... | collective-permute-start | bytes 6291464 | tf_op jit(solution)/shard_map/cond/branch_0_fun/ppermute | solution.py:46
  205.5 60.3 %collective-permute-start.20 = (bf16[8192,128]{1,0:T(8,128)(2,1)}, bf16[8192,128]{1,0:T(8,128)(2,1)}, u32[]{:S(2)}, u32[]{:S(2)}) collective-permute-start(bf16[8192,128]{1,0:T(8,128)(2,1)} %all-gather.12.cloned.1.call-done.refs_4_.refs_6_.refs_8_.refs_10_), channel_id=1, source_target_pairs={{0,1},{1,0},{2,3},{3,2},{4,5},{5,4},{6,7},{7,6},{8,9},{9,8},{10,11... | collective-permute-start | bytes 6291464 | tf_op jit(solution)/shard_map/cond/branch_0_fun/ppermute | solution.py:46
  207.5 21.2 %collective-permute-start.1 = (f32[192,128]{1,0:T(8,128)}, f32[192,128]{1,0:T(8,128)S(1)}, u32[]{:S(2)}, u32[]{:S(2)}) collective-permute-start(f32[192,128]{1,0:T(8,128)} %get-tuple-element.160), channel_id=1, source_target_pairs={{0,8},{4,12},{8,0},{12,4},{1,9},{5,13},{9,1},{13,5},{2,10},{6,14},... | collective-permute-start | bytes 294920 | tf_op jit(solution)/shard_map/cond/branch_0_fun/ppermute | solution.py:46
  207.7 33.3 %collective-permute-start.17 = (bf16[1536,256]{1,0:T(8,128)(2,1)}, bf16[1536,256]{1,0:T(8,128)(2,1)S(1)}, u32[]{:S(2)}, u32[]{:S(2)}) collective-permute-start(bf16[1536,256]{1,0:T(8,128)(2,1)} %stage.19.refs_0_), channel_id=1, source_target_pairs={{0,2},{1,3},{2,0},{3,1},{4,6},{5,7},{6,4},{7,5},{8,10},{9,11},{10,... | collective-permute-start | bytes 2359304 | tf_op jit(solution)/shard_map/cond/branch_0_fun/ppermute | solution.py:46
  227.7 35.6 %collective-permute-start.18 = (bf16[2048,256]{1,0:T(8,128)(2,1)}, bf16[2048,256]{1,0:T(8,128)(2,1)S(1)}, u32[]{:S(2)}, u32[]{:S(2)}) collective-permute-start(bf16[2048,256]{1,0:T(8,128)(2,1)} %get-tuple-element.93.refs_0_.refs_25_), channel_id=1, source_target_pairs={{0,2},{1,3},{2,0},{3,1},{4,6},{5,7},{6,4},{7,5},{8,10},{9,11},{10,... | collective-permute-start | bytes 3145736 | tf_op jit(solution)/shard_map/cond/branch_0_fun/ppermute | solution.py:46
  228.8 6.6 %copy-start.42 = (f32[192,128]{1,0:T(8,128)}, f32[192,128]{1,0:T(8,128)S(1)}, u32[]{:S(2)}) copy-start(f32[192,128]{1,0:T(8,128)S(1)} %collective-permute-done.1.c) | copy-start | bytes 294916 | tf_op jit(solution)/shard_map/cond
  228.8 6.5 %collective-permute-start.2 = (f32[192,128]{1,0:T(8,128)S(1)}, f32[192,128]{1,0:T(8,128)S(1)}, u32[]{:S(2)}, u32[]{:S(2)}) collective-permute-start(f32[192,128]{1,0:T(8,128)S(1)} %get-tuple-element.159), channel_id=1, source_target_pairs={{0,12},{4,8},{8,4},{12,0},{1,13},{5,9},{9,5},{13,1},{2,14},{6,10},... | collective-permute-start | bytes 294920 | tf_op jit(solution)/shard_map/cond/branch_0_fun/ppermute | solution.py:46
  238.4 19.1 %copy-start.29 = (f32[64,128]{1,0:T(8,128)}, f32[64,128]{1,0:T(8,128)S(1)}, u32[]{:S(2)}) copy-start(f32[64,128]{1,0:T(8,128)S(1)} %slice.18.a) | copy-start | bytes 98308 | tf_op jit(solution)/shard_map/cond
  238.4 21.0 %copy-start.17 = (f32[192,128]{1,0:T(8,128)S(1)}, f32[192,128]{1,0:T(8,128)}, u32[]{:S(2)}) copy-start(f32[192,128]{1,0:T(8,128)} %sum_parts.2.refs_26_) | copy-start | bytes 294916 | tf_op jit(solution)/shard_map/cond
  238.4 21.2 %copy-start.34 = (f32[128,256]{1,0:T(8,128)S(1)}, f32[128,256]{1,0:T(8,128)}, u32[]{:S(2)}) copy-start(f32[128,256]{1,0:T(8,128)} %get-tuple-element.95) | copy-start | bytes 393220 | tf_op jit(solution)/shard_map/cond
  238.4 19.1 %collective-permute-start.14 = (f32[64,128]{1,0:T(8,128)S(1)}, f32[64,128]{1,0:T(8,128)S(1)}, u32[]{:S(2)}, u32[]{:S(2)}) collective-permute-start(f32[64,128]{1,0:T(8,128)S(1)} %slice.18.a), channel_id=1, source_target_pairs={{0,4},{4,0},{8,12},{12,8},{1,5},{5,1},{9,13},{13,9},{2,6},{6,2},{1... | collective-permute-start | bytes 98312 | tf_op jit(solution)/shard_map/cond/branch_0_fun/ppermute | solution.py:46
  241.0 20.2 %collective-permute-start.15 = (f32[64,128]{1,0:T(8,128)S(1)}, f32[64,128]{1,0:T(8,128)S(1)}, u32[]{:S(2)}, u32[]{:S(2)}) collective-permute-start(f32[64,128]{1,0:T(8,128)S(1)} %slice.18.a), channel_id=1, source_target_pairs={{0,8},{4,12},{8,0},{12,4},{1,9},{5,13},{9,1},{13,5},{2,10},{6,14},... | collective-permute-start | bytes 98312 | tf_op jit(solution)/shard_map/cond/branch_0_fun/ppermute | solution.py:46
  257.5 5.8 %collective-permute-start.16 = (f32[64,128]{1,0:T(8,128)S(1)}, f32[64,128]{1,0:T(8,128)S(1)}, u32[]{:S(2)}, u32[]{:S(2)}) collective-permute-start(f32[64,128]{1,0:T(8,128)S(1)} %slice.18.a), channel_id=1, source_target_pairs={{0,12},{4,8},{8,4},{12,0},{1,13},{5,9},{9,5},{13,1},{2,14},{6,10},... | collective-permute-start | bytes 98312 | tf_op jit(solution)/shard_map/cond/branch_0_fun/ppermute | solution.py:46
  261.2 23.9 %collective-permute-start.22 = (bf16[1536,256]{1,0:T(8,128)(2,1)}, bf16[1536,256]{1,0:T(8,128)(2,1)S(1)}, u32[]{:S(2)}, u32[]{:S(2)}) collective-permute-start(bf16[1536,256]{1,0:T(8,128)(2,1)} %get-tuple-element.94.refs_0_.refs_25_), channel_id=1, source_target_pairs={{0,2},{1,3},{2,0},{3,1},{4,6},{5,7},{6,4},{7,5},{8,10},{9,11},{10,... | collective-permute-start | bytes 2359304 | tf_op jit(solution)/shard_map/cond/branch_0_fun/ppermute | solution.py:46
  265.8 37.6 %collective-permute-start.19 = (f32[64,512]{1,0:T(8,128)}, f32[64,512]{1,0:T(8,128)S(1)}, u32[]{:S(2)}, u32[]{:S(2)}) collective-permute-start(f32[64,512]{1,0:T(8,128)} %join_parts.2.refs_26_), channel_id=1, source_target_pairs={{0,1},{1,0},{2,3},{3,2},{4,5},{5,4},{6,7},{7,6},{8,9},{9,8},{10,11... | collective-permute-start | bytes 393224 | tf_op jit(solution)/shard_map/cond/branch_0_fun/ppermute | solution.py:46
  284.1 18.3 %copy-start.38 = (f32[128,256]{1,0:T(8,128)S(1)}, f32[128,256]{1,0:T(8,128)}, u32[]{:S(2)}) copy-start(f32[128,256]{1,0:T(8,128)} %get-tuple-element.99) | copy-start | bytes 393220 | tf_op jit(solution)/shard_map/cond
  284.1 19.3 %copy-start.23 = (f32[64,512]{1,0:T(8,128)S(1)}, f32[64,512]{1,0:T(8,128)}, u32[]{:S(2)}) copy-start(f32[64,512]{1,0:T(8,128)} %join_parts.2.refs_26_) | copy-start | bytes 393220 | tf_op jit(solution)/shard_map/cond
  284.1 19.3 %copy-start.53 = (s32[1,1024]{1,0:T(1,128)S(1)}, s32[1,1024]{1,0:T(1,128)}, u32[]{:S(2)}) copy-start(s32[1,1024]{1,0:T(1,128)} %copy-done.52) | copy-start | bytes 12292 | tf_op jit(solution)/shard_map/cond
  284.1 26.2 %collective-permute-start.23 = (bf16[2048,256]{1,0:T(8,128)(2,1)}, bf16[2048,256]{1,0:T(8,128)(2,1)S(1)}, u32[]{:S(2)}, u32[]{:S(2)}) collective-permute-start(bf16[2048,256]{1,0:T(8,128)(2,1)} %get-tuple-element.100.refs_25_), channel_id=1, source_target_pairs={{0,2},{1,3},{2,0},{3,1},{4,6},{5,7},{6,4},{7,5},{8,10},{9,11},{10,... | collective-permute-start | bytes 3145736 | tf_op jit(solution)/shard_map/cond/branch_0_fun/ppermute | solution.py:46
  301.2 25.6 %collective-permute-start.24 = (bf16[1536,256]{1,0:T(8,128)(2,1)}, bf16[1536,256]{1,0:T(8,128)(2,1)S(1)}, u32[]{:S(2)}, u32[]{:S(2)}) collective-permute-start(bf16[1536,256]{1,0:T(8,128)(2,1)} %get-tuple-element.104.refs_17_), channel_id=1, source_target_pairs={{0,2},{1,3},{2,0},{3,1},{4,6},{5,7},{6,4},{7,5},{8,10},{9,11},{10,... | collective-permute-start | bytes 2359304 | tf_op jit(solution)/shard_map/cond/branch_0_fun/ppermute | solution.py:46
  324.7 14.2 %copy-start.8 = (f32[128,256]{1,0:T(8,128)S(1)}, f32[128,256]{1,0:T(8,128)}, u32[]{:S(2)}) copy-start(f32[128,256]{1,0:T(8,128)} %stage.24.refs_17_) | copy-start | bytes 393220 | tf_op jit(solution)/shard_map/cond
  324.7 15.1 %copy-start.32 = (f32[128,256]{1,0:T(8,128)S(1)}, f32[128,256]{1,0:T(8,128)}, u32[]{:S(2)}) copy-start(f32[128,256]{1,0:T(8,128)} %add.173) | copy-start | bytes 393220 | tf_op jit(solution)/shard_map/cond
  324.7 15.1 %copy-start.60 = (f32[64,768]{1,0:T(8,128)S(1)}, f32[64,768]{1,0:T(8,128)}, u32[]{:S(2)}) copy-start(f32[64,768]{1,0:T(8,128)} %fusion.7) | copy-start | bytes 589828 | tf_op jit(solution)/shard_map/cond
  324.7 15.1 %copy-start.61 = (f32[8,768]{1,0:T(8,128)S(1)}, f32[8,768]{1,0:T(8,128)}, u32[]{:S(2)}) copy-start(f32[8,768]{1,0:T(8,128)} %fusion.8) | copy-start | bytes 73732 | tf_op jit(solution)/shard_map/cond
  352.2 6.9 %collective-permute-start.60 = (f32[8,16,192]{2,1,0:T(8,128)S(1)}, f32[8,16,192]{2,1,0:T(8,128)S(1)}, u32[]{:S(2)}, u32[]{:S(2)}) collective-permute-start(f32[8,16,192]{2,1,0:T(8,128)S(1)} %get-tuple-element.171), channel_id=1, source_target_pairs={{0,4},{4,0},{8,12},{12,8},{1,5},{5,1},{9,13},{13,9},{2,6},{6,2},{1... | collective-permute-start | bytes 294920 | tf_op jit(solution)/shard_map/ppermute | solution.py:46
  352.2 12.9 %collective-permute-start.61 = (f32[8,16,192]{2,1,0:T(8,128)S(1)}, f32[8,16,192]{2,1,0:T(8,128)S(1)}, u32[]{:S(2)}, u32[]{:S(2)}) collective-permute-start(f32[8,16,192]{2,1,0:T(8,128)S(1)} %get-tuple-element.173), channel_id=1, source_target_pairs={{0,8},{4,12},{8,0},{12,4},{1,9},{5,13},{9,1},{13,5},{2,10},{6,14},... | collective-permute-start | bytes 294920 | tf_op jit(solution)/shard_map/ppermute | solution.py:46
  354.6 10.5 %collective-permute-start.62 = (f32[8,16,192]{2,1,0:T(8,128)S(1)}, f32[8,16,192]{2,1,0:T(8,128)S(1)}, u32[]{:S(2)}, u32[]{:S(2)}) collective-permute-start(f32[8,16,192]{2,1,0:T(8,128)S(1)} %get-tuple-element.172), channel_id=1, source_target_pairs={{0,12},{4,8},{8,4},{12,0},{1,13},{5,9},{9,5},{13,1},{2,14},{6,10},... | collective-permute-start | bytes 294920 | tf_op jit(solution)/shard_map/ppermute | solution.py:46
  365.2 2.0 collective-permute-start.63
  365.3 6.4 %collective-permute-start.64 = (f32[8,16,192]{2,1,0:T(8,128)S(1)}, f32[8,16,192]{2,1,0:T(8,128)S(1)}, u32[]{:S(2)}, u32[]{:S(2)}) collective-permute-start(f32[8,16,192]{2,1,0:T(8,128)S(1)} %add_add_fusion.1), channel_id=1, source_target_pairs={{0,2},{1,3},{2,0},{3,1},{4,6},{5,7},{6,4},{7,5},{8,10},{9,11},{10,... | collective-permute-start | bytes 294920 | tf_op jit(solution)/shard_map/ppermute | solution.py:46
  366.3 7.2 %collective-permute-start.65 = (f32[8,16,192]{2,1,0:T(8,128)S(1)}, f32[8,16,192]{2,1,0:T(8,128)S(1)}, u32[]{:S(2)}, u32[]{:S(2)}) collective-permute-start(f32[8,16,192]{2,1,0:T(8,128)S(1)} %add_add_fusion.1), channel_id=1, source_target_pairs={{0,3},{1,2},{2,1},{3,0},{4,7},{5,6},{6,5},{7,4},{8,11},{9,10},{10,... | collective-permute-start | bytes 294920 | tf_op jit(solution)/shard_map/ppermute | solution.py:46
  375.5 1.9 collective-permute-start.66
  375.9 3.6 collective-permute-start.67
  376.9 3.0 collective-permute-start.68
  379.9 4.5 %collective-permute-start.69 = (f32[8,128]{1,0:T(8,128)S(1)}, f32[8,128]{1,0:T(8,128)S(1)}, u32[]{:S(2)}, u32[]{:S(2)}) collective-permute-start(f32[8,128]{1,0:T(8,128)S(1)} %add_add_fusion.2), channel_id=1, source_target_pairs={{0,4},{4,0},{8,12},{12,8},{1,5},{5,1},{9,13},{13,9},{2,6},{6,2},{1... | collective-permute-start | bytes 12296 | tf_op jit(solution)/shard_map/ppermute | solution.py:46
  382.0 4.5 %collective-permute-start.70 = (f32[8,128]{1,0:T(8,128)S(1)}, f32[8,128]{1,0:T(8,128)S(1)}, u32[]{:S(2)}, u32[]{:S(2)}) collective-permute-start(f32[8,128]{1,0:T(8,128)S(1)} %add_add_fusion.2), channel_id=1, source_target_pairs={{0,8},{4,12},{8,0},{12,4},{1,9},{5,13},{9,1},{13,5},{2,10},{6,14},... | collective-permute-start | bytes 12296 | tf_op jit(solution)/shard_map/ppermute | solution.py:46
  382.8 5.4 %collective-permute-start.71 = (f32[8,128]{1,0:T(8,128)S(1)}, f32[8,128]{1,0:T(8,128)S(1)}, u32[]{:S(2)}, u32[]{:S(2)}) collective-permute-start(f32[8,128]{1,0:T(8,128)S(1)} %add_add_fusion.2), channel_id=1, source_target_pairs={{0,12},{4,8},{8,4},{12,0},{1,13},{5,9},{9,5},{13,1},{2,14},{6,10},... | collective-permute-start | bytes 12296 | tf_op jit(solution)/shard_map/ppermute | solution.py:46
  (14 other events, 36.3 us)
Sparse Core Ops, SparseCore 0:
  31.7 47.1 all-gather.9
  83.8 50.4 all-gather.7
  135.9 58.2 all-gather.11
where the time goes:
time: 399 us; the launch traced here: 396 us
  Pallas kernels  155 us (39%)
  waiting for transfers between devices  107 us (27%)
  starting transfers between devices  66.3 us (17%)
  matrix products  18.7 us (5%)
  between operations  17.6 us (4%)
  other arithmetic  11.8 us (3%)
  loops' own time  11.3 us (3%)
  local copies, waits for them, and re-layouts  8.11 us (2%)
    pallas_call x8, Pallas kernels, stage(): pl.pallas_call(functools.partial(stage_kernel, far is not None, own is no...  113 us
    ppermute x39, waiting for transfers between devices, swap(): return lax.ppermute(array, axis, [(i, i ^ bits) for i in range(count)])  59.5 us
    ppermute x39, starting transfers between devices, swap(): return lax.ppermute(array, axis, [(i, i ^ bits) for i in range(count)])  57.1 us
    all_gather x2, waiting for transfers between devices, packed_scores(): lax.all_gather(blocks[k], 'tensor', axis=0, tiled=True)  32.1 us
    pallas_call x3, Pallas kernels, pack(): pl.pallas_call(functools.partial(pack_kernel, size, count), grid_spec=plt...  26.8 us
    ppermute x2, waiting for transfers between devices, move(): return lax.ppermute(array, ('tensor', 'example'), pairs)  14.8 us
    dot_general x4, matrix products, contract(): lax.dot_general(left_side, right_side, (((1,), (1,)), ((), ())), preferre...  12.9 us
    another operation x1, loops' own time, local_four(): lax.switch(branch, [functools.partial(packed_scores, level) for level in...  11.3 us
  transfers between devices with their start and end apart: 45, of which 18 were waited for; matrix products, arithmetic and copies ran while one was open for 7% of the time, Pallas kernels for 35%

commit v1 on v0

--- a/solution.py
+++ b/solution.py
@@ -424,8 +424,6 @@
 
     came, right, after = [], [], ()
     for h, tiles in enumerate(tile_parts):
-        if h == 1:
-            after += tuple(shards)
         results = run(h, far_pair, None, after)
         came.append((swap(results[0], "example", 2), tiles[0]))
         after = (results[0],)
@@ -434,7 +432,7 @@
         if k == 1:
             away = cut(1 - far_at, gathered[1], after)
             far_next = swap(away, "example", 2)
-            after = (away, came[0][0])
+            after = (away, came[0][0], *shards)
             gate_packed = pack(chunks, 2 * LANES, half_hidden, offset, place, gate_rows, gate_near, after)
             up_packed = pack(chunks, 2 * LANES, half_hidden, offset, place, up_rows, up_near, after)
             after = (gate_packed[0], up_packed[0])

time: 399 us -> 399 us (level)
  no operation moved by 1% of the time
where the time goes in v1:
time: 399 us; the launch traced here: 396 us
  Pallas kernels  155 us (39%)
  waiting for transfers between devices  107 us (27%)
  starting transfers between devices  66.3 us (17%)
  matrix products  18.7 us (5%)
  between operations  17.6 us (4%)
  other arithmetic  11.8 us (3%)
  loops' own time  11.3 us (3%)
  local copies, waits for them, and re-layouts  8.11 us (2%)
    pallas_call x8, Pallas kernels, stage(): pl.pallas_call(functools.partial(stage_kernel, far is not None, own is no...  113 us
    ppermute x39, waiting for transfers between devices, swap(): return lax.ppermute(array, axis, [(i, i ^ bits) for i in range(count)])  59.5 us
    ppermute x39, starting transfers between devices, swap(): return lax.ppermute(array, axis, [(i, i ^ bits) for i in range(count)])  57.1 us
    all_gather x2, waiting for transfers between devices, packed_scores(): lax.all_gather(blocks[k], 'tensor', axis=0, tiled=True)  32.1 us
    pallas_call x3, Pallas kernels, pack(): pl.pallas_call(functools.partial(pack_kernel, size, count), grid_spec=plt...  26.8 us
    ppermute x2, waiting for transfers between devices, move(): return lax.ppermute(array, ('tensor', 'example'), pairs)  14.8 us
    dot_general x4, matrix products, contract(): lax.dot_general(left_side, right_side, (((1,), (1,)), ((), ())), preferre...  12.9 us
    another operation x1, loops' own time, local_four(): lax.switch(branch, [functools.partial(packed_scores, level) for level in...  11.3 us
  transfers between devices with their start and end apart: 45, of which 18 were waited for; matrix products, arithmetic and copies ran while one was open for 7% of the time, Pallas kernels for 35%

profile of v1, /device:TPU:0, one launch (start us, length us, event | category | flops | bytes accessed | tf_op | source)
XLA Modules:
  0.0 395.6 jit_solution(4642336133712426485)
XLA Ops:
  7.0 2.9 collective-permute-start.56
  12.2 1.3 bitcast_subtract_fusion.1
  17.8 3.9 collective-permute-start.58
  23.2 6.0 %pack_rows.9 = (bf16[2048,128]{1,0:T(8,128)(2,1)}, bf16[2048,128]{1,0:T(8,128)(2,1)}, bf16[2048,128]{1,0:T(8,128)(2,1)}, bf16[2048,128]{1,0:T(8,128)(2,1)}) custom-call(s32[1]{0:T(128)} %constant.189.clone.1.near_ref, s32[1,1024]{1,0:T(1,128)S(1)} %bitcast.71, bf16[512,2048]{1,0:T(8,128)(2,1)} %bitcast.68, bf16[512,2048]{1,0:T(8,128)(2,1)} %collective-permute-done.59.other_ref), custom_call_target="tpu_custom_call" | custom-call | flops 2147483648 | bytes 6291456 | tf_op jit(solution)/shard_map/pack_rows/pallas_call | solution.py:94
  29.3 322.9 %conditional.1 = (f32[8,64,192]{2,1,0:T(8,128)S(1)}) conditional(s32[]{:T(128)} %bitcast.25, (s32[16]{0:T(128)S(1)}, s32[1,1024]{1,0:T(1,128)S(1)}, bf16[4,128,2048]{2,1,0:T(8,128)(2,1)}, bf16[64,2048]{1,0:T(8,128)(2,1)}, bf16[4,128,7168]{2,1,0:T(8,128)(2,1)}, /*index=5*/bf16[4,128,7168]{2,1,0:T(8,128)(2,1)}, bf16[64,7168]{1,0:T(8,128)(2,1)}, ...), branch_computations={%region_6.7_spmd, %region_7.8_spmd} | conditional | flops 77567238144 | bytes 580137728 | solution.py:536
  30.6 1.3 collective-permute-start.4
  31.9 14.8 %collective-permute-done.4.refs_0_.b = bf16[2048,128]{1,0:T(8,128)(2,1)} collective-permute-done((bf16[2048,128]{1,0:T(8,128)(2,1)}, bf16[2048,128]{1,0:T(8,128)(2,1)}, u32[]{:S(2)}, u32[]{:S(2)}) %collective-permute-start.4) | collective-permute-done | bytes 524320 | tf_op jit(solution)/shard_map/cond/branch_0_fun/ppermute | solution.py:65
  46.8 32.1 %all-gather.10.cloned.1.call-done.source.refs_12_.refs_14_.refs_16_.refs_18_ = bf16[8192,128]{1,0:T(8,128)(2,1)} async-done(((bf16[2048,128]{1,0:T(8,128)(2,1)}), bf16[8192,128]{1,0:T(8,128)(2,1)}) %all-gather.10.cloned.1.call-update) | async-done | bytes 2097168 | tf_op jit(solution)/shard_map/cond/branch_0_fun/all_gather | solution.py:383
  78.8 3.4 cut_columns.4.refs_0_
  82.2 1.5 collective-permute-start.5
  83.8 2.3 pair_halves.3
  86.1 3.9 collective-permute-start.10
  90.0 17.5 %collective-permute-done.5.refs_4_.refs_6_.refs_8_.refs_10_ = bf16[4096,128]{1,0:T(8,128)(2,1)} collective-permute-done((bf16[4096,128]{1,0:T(8,128)(2,1)}, bf16[4096,128]{1,0:T(8,128)(2,1)}, u32[]{:S(2)}, u32[]{:S(2)}) %collective-permute-start.5) | collective-permute-done | bytes 1048608 | tf_op jit(solution)/shard_map/cond/branch_0_fun/ppermute | solution.py:46
  107.4 8.5 %fusion.13 = f32[64,512]{1,0:T(8,128)} fusion(bf16[64,7168]{1,0:T(8,128)(2,1)S(1)} %copy-done.59, bf16[512,7168]{1,0:T(8,128)(2,1)} %bitcast.87, bf16[512,7168]{1,0:T(8,128)(2,1)} %bitcast.81), kind=kOutput, calls=%fused_computation.15 | convolution fusion | flops 499122176 | bytes 15728640 | tf_op jit(solution)/shard_map/cond/branch_0_fun/dot_general | solution.py:18
  116.6 2.4 fusion.89
  120.0 11.8 %stage.18.refs_12_ = bf16[2048,256]{1,0:T(8,128)(2,1)} custom-call(s32[1]{0:T(128)} %bitcast.6.offset_ref.near_ref, s32[2]{0:T(128)} %pad_add_fusion.1.near_ref, bf16[7168,2048]{1,0:T(8,128)(2,1)} %get-tuple-element.83.refs_0_.refs_1_, bf16[7168,2048]{1,0:T(8,128)(2,1)} %get-tuple-element.83.refs_0_.refs_1_, ...), custom_call_target="tpu_custom_call" | custom-call | flops 4294967296 | bytes 18874368 | tf_op jit(solution)/shard_map/cond/branch_0_fun/stage/pallas_call | solution.py:321
  131.8 23.8 %collective-permute-start.9 = (bf16[2048,256]{1,0:T(8,128)(2,1)}, bf16[2048,256]{1,0:T(8,128)(2,1)}, u32[]{:S(2)}, u32[]{:S(2)}) collective-permute-start(bf16[2048,256]{1,0:T(8,128)(2,1)} %stage.18.refs_12_), channel_id=1, source_target_pairs={{0,2},{1,3},{2,0},{3,1},{4,6},{5,7},{6,4},{7,5},{8,10},{9,11},{10,... | collective-permute-start | bytes 3145736 | tf_op jit(solution)/shard_map/cond/branch_0_fun/ppermute | solution.py:46
  157.4 10.0 %stage.19.refs_0_ = bf16[1536,256]{1,0:T(8,128)(2,1)} custom-call(s32[1]{0:T(128)} %bitcast.6.offset_ref.near_ref, s32[2]{0:T(128)} %pad_add_fusion.1.near_ref, bf16[7168,2048]{1,0:T(8,128)(2,1)} %get-tuple-element.83.refs_0_.refs_1_, bf16[7168,2048]{1,0:T(8,128)(2,1)} %get-tuple-element.83.refs_0_.refs_1_, ...), custom_call_target="tpu_custom_call" | custom-call | flops 3221225472 | bytes 14155776 | tf_op jit(solution)/shard_map/cond/branch_0_fun/stage/pallas_call | solution.py:321
  167.4 3.4 cut_columns.5.refs_0_
  170.8 9.1 %collective-permute-done.9.refs_1_.refs_20_ = bf16[2048,256]{1,0:T(8,128)(2,1)} collective-permute-done((bf16[2048,256]{1,0:T(8,128)(2,1)}, bf16[2048,256]{1,0:T(8,128)(2,1)}, u32[]{:S(2)}, u32[]{:S(2)}) %collective-permute-start.9) | collective-permute-done | bytes 1048608 | tf_op jit(solution)/shard_map/cond/branch_0_fun/ppermute | solution.py:46
  179.9 10.4 %pack_rows.6 = (bf16[3584,256]{1,0:T(8,128)(2,1)}, bf16[3584,256]{1,0:T(8,128)(2,1)}, bf16[3584,256]{1,0:T(8,128)(2,1)}) custom-call(s32[1]{0:T(128)} %bitcast.6.offset_ref.near_ref, s32[1,1024]{1,0:T(1,128)S(1)} %get-tuple-element.75.place_ref, bf16[512,7168]{1,0:T(8,128)(2,1)} %bitcast.88, bf16[512,7168]{1,0:T(8,128)(2,1)} %collective-permute-done.11.other_ref, ...), custom_call_target="tpu_custom_call" | custom-call | flops 5637144576 | bytes 12845056 | tf_op jit(solution)/shard_map/cond/branch_0_fun/pack_rows/pallas_call | solution.py:94
  190.4 10.4 %pack_rows.5 = (bf16[3584,256]{1,0:T(8,128)(2,1)}, bf16[3584,256]{1,0:T(8,128)(2,1)}, bf16[3584,256]{1,0:T(8,128)(2,1)}) custom-call(s32[1]{0:T(128)} %bitcast.6.offset_ref.near_ref, s32[1,1024]{1,0:T(1,128)S(1)} %get-tuple-element.75.place_ref, bf16[512,7168]{1,0:T(8,128)(2,1)} %bitcast.82, bf16[512,7168]{1,0:T(8,128)(2,1)} %collective-permute-done.8.other_ref, ...), custom_call_target="tpu_custom_call" | custom-call | flops 5637144576 | bytes 12845056 | tf_op jit(solution)/shard_map/cond/branch_0_fun/pack_rows/pallas_call | solution.py:94
  201.5 1.0 copy-done.15
  202.4 2.3 ordered_copy.2.refs_4_.refs_6_.refs_8_.refs_10_
  206.3 1.2 fusion.8
  207.7 1.7 collective-permute-start.17
  209.4 18.3 %stage.20 = (bf16[2048,256]{1,0:T(8,128)(2,1)}, f32[128,256]{1,0:T(8,128)}) custom-call(s32[1]{0:T(128)} %bitcast.6.offset_ref.near_ref, s32[2]{0:T(128)} %pad_add_fusion.1.near_ref, bf16[7168,2048]{1,0:T(8,128)(2,1)} %get-tuple-element.83.refs_0_.refs_1_, bf16[7168,2048]{1,0:T(8,128)(2,1)} %get-tuple-element.83.refs_0_.refs_1_, ...), custom_call_target="tpu_custom_call" | custom-call | flops 8589934592 | bytes 20971520 | tf_op jit(solution)/shard_map/cond/branch_0_fun/stage/pallas_call | solution.py:321
  228.8 3.1 collective-permute-start.2
  231.9 3.4 collective-permute-done.2.d
  236.0 1.7 sum_parts.2.refs_26_
  238.4 2.6 collective-permute-start.14
  241.0 1.1 collective-permute-start.15
  242.1 15.4 %stage.21 = (bf16[1536,256]{1,0:T(8,128)(2,1)}, f32[128,256]{1,0:T(8,128)}) custom-call(s32[1]{0:T(128)} %bitcast.6.offset_ref.near_ref, s32[2]{0:T(128)} %pad_add_fusion.1.near_ref, bf16[7168,2048]{1,0:T(8,128)(2,1)} %get-tuple-element.83.refs_0_.refs_1_, bf16[7168,2048]{1,0:T(8,128)(2,1)} %get-tuple-element.83.refs_0_.refs_1_, ...), custom_call_target="tpu_custom_call" | custom-call | flops 6442450944 | bytes 15728640 | tf_op jit(solution)/shard_map/cond/branch_0_fun/stage/pallas_call | solution.py:321
  257.5 1.9 collective-permute-start.16
  259.6 1.6 add.173
  261.2 1.3 collective-permute-start.22
  264.3 1.5 join_parts.2.refs_26_
  265.8 18.3 %stage.22 = (bf16[2048,256]{1,0:T(8,128)(2,1)}, f32[128,256]{1,0:T(8,128)}) custom-call(s32[1]{0:T(128)} %bitcast.6.offset_ref.near_ref, s32[2]{0:T(128)} %pad_add_fusion.1.near_ref, bf16[7168,2048]{1,0:T(8,128)(2,1)} %get-tuple-element.83.refs_0_.refs_1_, bf16[7168,2048]{1,0:T(8,128)(2,1)} %get-tuple-element.83.refs_0_.refs_1_, ...), custom_call_target="tpu_custom_call" | custom-call | flops 8589934592 | bytes 20971520 | tf_op jit(solution)/shard_map/cond/branch_0_fun/stage/pallas_call | solution.py:321
  284.1 1.0 collective-permute-start.23
  286.1 15.1 %stage.23 = (bf16[1536,256]{1,0:T(8,128)(2,1)}, f32[128,256]{1,0:T(8,128)}) custom-call(s32[1]{0:T(128)} %bitcast.6.offset_ref.near_ref, s32[2]{0:T(128)} %pad_add_fusion.1.near_ref, bf16[7168,2048]{1,0:T(8,128)(2,1)} %get-tuple-element.83.refs_0_.refs_1_, bf16[7168,2048]{1,0:T(8,128)(2,1)} %get-tuple-element.83.refs_0_.refs_1_, ...), custom_call_target="tpu_custom_call" | custom-call | flops 6442450944 | bytes 15728640 | tf_op jit(solution)/shard_map/cond/branch_0_fun/stage/pallas_call | solution.py:321
  301.2 1.1 collective-permute-start.24
  302.4 0.9 add.174
  303.4 2.4 fusion.7
  305.8 4.6 %collective-permute-done.23.refs_12_ = bf16[2048,256]{1,0:T(8,128)(2,1)S(1)} collective-permute-done((bf16[2048,256]{1,0:T(8,128)(2,1)}, bf16[2048,256]{1,0:T(8,128)(2,1)S(1)}, u32[]{:S(2)}, u32[]{:S(2)}) %collective-permute-start.23) | collective-permute-done | bytes 1048608 | tf_op jit(solution)/shard_map/cond/branch_0_fun/ppermute | solution.py:46
  310.4 1.0 copy-done.11
  311.3 13.3 %stage.24.refs_17_ = f32[128,256]{1,0:T(8,128)} custom-call(s32[1]{0:T(128)} %bitcast.6.offset_ref.near_ref, s32[2]{0:T(128)} %pad_add_fusion.1.near_ref, bf16[7168,2048]{1,0:T(8,128)(2,1)} %get-tuple-element.83.refs_0_.refs_1_, bf16[7168,2048]{1,0:T(8,128)(2,1)} %get-tuple-element.83.refs_0_.refs_1_, ...), custom_call_target="tpu_custom_call" | custom-call | flops 4294967296 | bytes 18874368 | tf_op jit(solution)/shard_map/cond/branch_0_fun/stage/pallas_call | solution.py:321
  324.7 2.1 collective-permute-done.24.refs_12_
  327.7 11.2 %stage.25 = f32[128,256]{1,0:T(8,128)} custom-call(s32[1]{0:T(128)} %bitcast.6.offset_ref.near_ref, s32[2]{0:T(128)} %pad_add_fusion.1.near_ref, bf16[7168,2048]{1,0:T(8,128)(2,1)} %get-tuple-element.83.refs_0_.refs_1_, bf16[7168,2048]{1,0:T(8,128)(2,1)} %get-tuple-element.83.refs_0_.refs_1_, bf16[7168,2048]{1,0:T(8,128)(2,1)} %collective-permute-done.3.refs_2_.refs_3_, ...), custom_call_target="tpu_custom_call" | custom-call | flops 3221225472 | bytes 14155776 | tf_op jit(solution)/shard_map/cond/branch_0_fun/stage/pallas_call | solution.py:321
  338.9 0.9 add.175
  339.8 1.4 fusion.9
  352.2 2.4 collective-permute-start.61
  354.6 2.0 collective-permute-start.62
  356.6 2.4 collective-permute-done.60
  359.0 6.1 %collective-permute-done.61 = f32[8,16,192]{2,1,0:T(8,128)S(1)} collective-permute-done((f32[8,16,192]{2,1,0:T(8,128)S(1)}, f32[8,16,192]{2,1,0:T(8,128)S(1)}, u32[]{:S(2)}, u32[]{:S(2)}) %collective-permute-start.61) | collective-permute-done | bytes 98336 | tf_op jit(solution)/shard_map/ppermute | solution.py:46
  365.3 1.1 collective-permute-start.64
  367.2 4.5 %collective-permute-done.64 = f32[8,16,192]{2,1,0:T(8,128)S(1)} collective-permute-done((f32[8,16,192]{2,1,0:T(8,128)S(1)}, f32[8,16,192]{2,1,0:T(8,128)S(1)}, u32[]{:S(2)}, u32[]{:S(2)}) %collective-permute-start.64) | collective-permute-done | bytes 98336 | tf_op jit(solution)/shard_map/ppermute | solution.py:46
  371.6 1.9 collective-permute-done.65
  373.7 1.3 fusion.93
  375.9 1.0 collective-permute-start.67
  377.4 2.0 collective-permute-done.67
  379.9 2.1 collective-permute-start.69
  382.8 1.7 collective-permute-start.71
  384.5 2.1 collective-permute-done.70
  386.5 1.7 collective-permute-done.71
  (160 shorter events, 22.5 us)
Async XLA Ops:
  6.5 367.1 %copy-start = (bf16[256,3072]{1,0:T(8,128)(2,1)S(1)}, bf16[256,3072]{1,0:T(8,128)(2,1)}, u32[]{:S(2)}) copy-start(bf16[256,3072]{1,0:T(8,128)(2,1)} %param.27) | copy-start | bytes 4718596
  6.5 16.6 %collective-permute-start.59 = (bf16[512,2048]{1,0:T(8,128)(2,1)}, bf16[512,2048]{1,0:T(8,128)(2,1)}, u32[]{:S(2)}, u32[]{:S(2)}) collective-permute-start(bf16[512,2048]{1,0:T(8,128)(2,1)} %bitcast.67), channel_id=1, source_target_pairs={{0,1},{1,0},{2,3},{3,2},{4,5},{5,4},{6,7},{7,6},{8,9},{9,8},{10,11... | collective-permute-start | bytes 6291464 | tf_op jit(solution)/shard_map/ppermute | solution.py:46
  7.0 3.9 collective-permute-start.55
  7.0 8.3 %collective-permute-start.56 = (s32[4]{0:T(128)}, s32[4]{0:T(128)S(1)}, u32[]{:S(2)}, u32[]{:S(2)}) collective-permute-start(s32[4]{0:T(128)} %param.28), channel_id=1, source_target_pairs={{0,2},{1,3},{2,0},{3,1},{4,6},{5,7},{6,4},{7,5},{8,10},{9,11},{10,... | collective-permute-start | bytes 56 | tf_op jit(solution)/shard_map/ppermute | solution.py:46
  10.0 6.0 %collective-permute-start.57 = (s32[4]{0:T(128)}, s32[4]{0:T(128)S(1)}, u32[]{:S(2)}, u32[]{:S(2)}) collective-permute-start(s32[4]{0:T(128)} %param.28), channel_id=1, source_target_pairs={{0,3},{1,2},{2,1},{3,0},{4,7},{5,6},{6,5},{7,4},{8,11},{9,10},{10,... | collective-permute-start | bytes 56 | tf_op jit(solution)/shard_map/ppermute | solution.py:46
  17.8 4.8 %collective-permute-start.58 = (s32[1]{0:T(128)}, s32[1]{0:T(128)}, u32[]{:S(2)}, u32[]{:S(2)}) collective-permute-start(s32[1]{0:T(128)} %bitcast.24), channel_id=1, source_target_pairs={{0,16},{16,0},{1,17},{17,1},{2,18},{18,2},{3,19},{19,3},{4,20},{20... | collective-permute-start | bytes 20 | tf_op jit(solution)/shard_map/ppermute | solution.py:532
  23.2 6.0 %copy-start.2 = (bf16[64,7168]{1,0:T(8,128)(2,1)S(1)}, bf16[64,7168]{1,0:T(8,128)(2,1)}, u32[]{:S(2)}) copy-start(bf16[64,7168]{1,0:T(8,128)(2,1)} %param.25) | copy-start | bytes 2752516
  29.2 337.9 %copy-start.54 = (s32[256]{0:T(256)S(1)}, s32[256]{0:T(256)}, u32[]{:S(2)}) copy-start(s32[256]{0:T(256)} %param.30) | copy-start | bytes 3076
  29.3 177.0 %copy-start.52 = (s32[1,1024]{1,0:T(1,128)}, s32[1,1024]{1,0:T(1,128)S(1)}, u32[]{:S(2)}) copy-start(s32[1,1024]{1,0:T(1,128)S(1)} %get-tuple-element.75.place_ref) | copy-start | bytes 12292 | tf_op jit(solution)/shard_map/cond
  29.3 49.6 %all-gather.10.cloned.1.call-start = ((), (), s32[]{:S(2)}) async-start(), calls=%async_computation.1 | async-start | bytes 2621440 | tf_op jit(solution)/shard_map/cond/branch_0_fun/all_gather | solution.py:383
  29.3 90.6 %collective-permute-start.3 = (bf16[7168,2048]{1,0:T(8,128)(2,1)}, bf16[7168,2048]{1,0:T(8,128)(2,1)}, u32[]{:S(2)}, u32[]{:S(2)}) collective-permute-start(bf16[7168,2048]{1,0:T(8,128)(2,1)} %get-tuple-element.83.refs_0_.refs_1_), channel_id=1, source_target_pairs={{0,1},{1,0},{2,3},{3,2},{4,5},{5,4},{6,7},{7,6},{8,9},{9,8},{10,11... | collective-permute-start | bytes 88080392 | tf_op jit(solution)/shard_map/cond/branch_0_fun/ppermute | solution.py:46
  30.0 137.4 %all-gather.8.cloned.1.call-start = ((), (), s32[]{:S(2)}) async-start(), calls=%async_computation | async-start | bytes 2621440 | tf_op jit(solution)/shard_map/cond/branch_0_fun/all_gather | solution.py:383
  30.1 140.7 %collective-permute-start.11 = (bf16[512,7168]{1,0:T(8,128)(2,1)}, bf16[512,7168]{1,0:T(8,128)(2,1)}, u32[]{:S(2)}, u32[]{:S(2)}) collective-permute-start(bf16[512,7168]{1,0:T(8,128)(2,1)} %bitcast.86), channel_id=1, source_target_pairs={{0,1},{1,0},{2,3},{3,2},{4,5},{5,4},{6,7},{7,6},{8,9},{9,8},{10,11... | collective-permute-start | bytes 22020104 | tf_op jit(solution)/shard_map/cond/branch_0_fun/ppermute | solution.py:46
  30.1 160.2 %collective-permute-start.8 = (bf16[512,7168]{1,0:T(8,128)(2,1)}, bf16[512,7168]{1,0:T(8,128)(2,1)}, u32[]{:S(2)}, u32[]{:S(2)}) collective-permute-start(bf16[512,7168]{1,0:T(8,128)(2,1)} %bitcast.80), channel_id=1, source_target_pairs={{0,1},{1,0},{2,3},{3,2},{4,5},{5,4},{6,7},{7,6},{8,9},{9,8},{10,11... | collective-permute-start | bytes 22020104 | tf_op jit(solution)/shard_map/cond/branch_0_fun/ppermute | solution.py:46
  30.6 16.1 %collective-permute-start.4 = (bf16[2048,128]{1,0:T(8,128)(2,1)}, bf16[2048,128]{1,0:T(8,128)(2,1)}, u32[]{:S(2)}, u32[]{:S(2)}) collective-permute-start(bf16[2048,128]{1,0:T(8,128)(2,1)} %get-tuple-element.86.a), channel_id=1, source_target_pairs={{2,0},{3,1},{6,4},{7,5},{8,10},{9,11},{12,14},{13,15},{18,16},{19,... | collective-permute-start | bytes 1572872 | tf_op jit(solution)/shard_map/cond/branch_0_fun/ppermute | solution.py:65
  82.2 25.2 %collective-permute-start.5 = (bf16[4096,128]{1,0:T(8,128)(2,1)}, bf16[4096,128]{1,0:T(8,128)(2,1)}, u32[]{:S(2)}, u32[]{:S(2)}) collective-permute-start(bf16[4096,128]{1,0:T(8,128)(2,1)} %cut_columns.4.refs_0_), channel_id=1, source_target_pairs={{0,2},{1,3},{2,0},{3,1},{4,6},{5,7},{6,4},{7,5},{8,10},{9,11},{10,... | collective-permute-start | bytes 3145736 | tf_op jit(solution)/shard_map/cond/branch_0_fun/ppermute | solution.py:46
  83.7 121.7 %all-gather.12.cloned.1.call-start = ((), (), s32[]{:S(2)}) async-start(), calls=%async_computation.2 | async-start | bytes 2621440 | tf_op jit(solution)/shard_map/cond/branch_0_fun/all_gather | solution.py:423
  83.8 23.7 %copy-start.59 = (bf16[64,7168]{1,0:T(8,128)(2,1)S(1)}, bf16[64,7168]{1,0:T(8,128)(2,1)}, u32[]{:S(2)}) copy-start(bf16[64,7168]{1,0:T(8,128)(2,1)} %get-tuple-element.80) | copy-start | bytes 2752516 | tf_op jit(solution)/shard_map/cond
  86.1 32.9 %collective-permute-start.10 = (bf16[2048,128]{1,0:T(8,128)(2,1)}, bf16[2048,128]{1,0:T(8,128)(2,1)}, u32[]{:S(2)}, u32[]{:S(2)}) collective-permute-start(bf16[2048,128]{1,0:T(8,128)(2,1)} %get-tuple-element.88), channel_id=1, source_target_pairs={{0,8},{1,9},{4,12},{5,13},{10,2},{11,3},{14,6},{15,7},{16,24},{17,... | collective-permute-start | bytes 1572872 | tf_op jit(solution)/shard_map/cond/branch_0_fun/ppermute | solution.py:65
  107.4 12.5 %collective-permute-start.6 = (bf16[4096,128]{1,0:T(8,128)(2,1)}, bf16[4096,128]{1,0:T(8,128)(2,1)}, u32[]{:S(2)}, u32[]{:S(2)}) collective-permute-start(bf16[4096,128]{1,0:T(8,128)(2,1)} %collective-permute-done.5.refs_4_.refs_6_.refs_8_.refs_10_), channel_id=1, source_target_pairs={{0,1},{1,0},{2,3},{3,2},{4,5},{5,4},{6,7},{7,6},{8,9},{9,8},{10,11... | collective-permute-start | bytes 3145736 | tf_op jit(solution)/shard_map/cond/branch_0_fun/ppermute | solution.py:46
  120.0 35.7 %copy-start.4 = (bf16[512,2048]{1,0:T(8,128)(2,1)S(1)}, bf16[512,2048]{1,0:T(8,128)(2,1)}, u32[]{:S(2)}) copy-start(bf16[512,2048]{1,0:T(8,128)(2,1)} %get-tuple-element.82) | copy-start | bytes 6291460 | tf_op jit(solution)/shard_map/cond
  120.0 35.6 %copy-start.12 = (bf16[64,2048]{1,0:T(8,128)(2,1)S(1)}, bf16[64,2048]{1,0:T(8,128)(2,1)}, u32[]{:S(2)}) copy-start(bf16[64,2048]{1,0:T(8,128)(2,1)} %get-tuple-element.81) | copy-start | bytes 786436 | tf_op jit(solution)/shard_map/cond
  131.8 24.6 %copy-start.41 = (f32[64,512]{1,0:T(8,128)S(1)}, f32[64,512]{1,0:T(8,128)}, u32[]{:S(2)}) copy-start(f32[64,512]{1,0:T(8,128)} %fusion.13) | copy-start | bytes 393220 | tf_op jit(solution)/shard_map/cond
  131.8 48.1 %collective-permute-start.9 = (bf16[2048,256]{1,0:T(8,128)(2,1)}, bf16[2048,256]{1,0:T(8,128)(2,1)}, u32[]{:S(2)}, u32[]{:S(2)}) collective-permute-start(bf16[2048,256]{1,0:T(8,128)(2,1)} %stage.18.refs_12_), channel_id=1, source_target_pairs={{0,2},{1,3},{2,0},{3,1},{4,6},{5,7},{6,4},{7,5},{8,10},{9,11},{10,... | collective-permute-start | bytes 3145736 | tf_op jit(solution)/shard_map/cond/branch_0_fun/ppermute | solution.py:46
  157.2 70.5 %collective-permute-start = (f32[192,128]{1,0:T(8,128)}, f32[192,128]{1,0:T(8,128)}, u32[]{:S(2)}, u32[]{:S(2)}) collective-permute-start(f32[192,128]{1,0:T(8,128)} %get-tuple-element.161), channel_id=1, source_target_pairs={{0,4},{4,0},{8,12},{12,8},{1,5},{5,1},{9,13},{13,9},{2,6},{6,2},{1... | collective-permute-start | bytes 294920 | tf_op jit(solution)/shard_map/cond/branch_0_fun/ppermute | solution.py:46
  157.4 50.2 %collective-permute-start.13 = (bf16[8192,128]{1,0:T(8,128)(2,1)}, bf16[8192,128]{1,0:T(8,128)(2,1)}, u32[]{:S(2)}, u32[]{:S(2)}) collective-permute-start(bf16[8192,128]{1,0:T(8,128)(2,1)} %all-gather.10.cloned.1.call-done.source.refs_12_.refs_14_.refs_16_.refs_18_), channel_id=1, source_target_pairs={{0,1},{1,0},{2,3},{3,2},{4,5},{5,4},{6,7},{7,6},{8,9},{9,8},{10,11... | collective-permute-start | bytes 6291464 | tf_op jit(solution)/shard_map/cond/branch_0_fun/ppermute | solution.py:46
  170.7 30.7 %collective-permute-start.7 = (bf16[4096,128]{1,0:T(8,128)(2,1)}, bf16[4096,128]{1,0:T(8,128)(2,1)S(1)}, u32[]{:S(2)}, u32[]{:S(2)}) collective-permute-start(bf16[4096,128]{1,0:T(8,128)(2,1)} %cut_columns.5.refs_0_), channel_id=1, source_target_pairs={{0,2},{1,3},{2,0},{3,1},{4,6},{5,7},{6,4},{7,5},{8,10},{9,11},{10,... | collective-permute-start | bytes 3145736 | tf_op jit(solution)/shard_map/cond/branch_0_fun/ppermute | solution.py:46
  204.7 3.0 collective-permute-start.12
  204.9 60.9 %collective-permute-start.21 = (bf16[8192,128]{1,0:T(8,128)(2,1)}, bf16[8192,128]{1,0:T(8,128)(2,1)}, u32[]{:S(2)}, u32[]{:S(2)}) collective-permute-start(bf16[8192,128]{1,0:T(8,128)(2,1)} %all-gather.8.cloned.1.call-done.source.refs_12_.refs_14_.refs_16_.refs_18_), channel_id=1, source_target_pairs={{0,1},{1,0},{2,3},{3,2},{4,5},{5,4},{6,7},{7,6},{8,9},{9,8},{10,11... | collective-permute-start | bytes 6291464 | tf_op jit(solution)/shard_map/cond/branch_0_fun/ppermute | solution.py:46
  205.5 60.3 %collective-permute-start.20 = (bf16[8192,128]{1,0:T(8,128)(2,1)}, bf16[8192,128]{1,0:T(8,128)(2,1)}, u32[]{:S(2)}, u32[]{:S(2)}) collective-permute-start(bf16[8192,128]{1,0:T(8,128)(2,1)} %all-gather.12.cloned.1.call-done.refs_4_.refs_6_.refs_8_.refs_10_), channel_id=1, source_target_pairs={{0,1},{1,0},{2,3},{3,2},{4,5},{5,4},{6,7},{7,6},{8,9},{9,8},{10,11... | collective-permute-start | bytes 6291464 | tf_op jit(solution)/shard_map/cond/branch_0_fun/ppermute | solution.py:46
  207.5 21.2 %collective-permute-start.1 = (f32[192,128]{1,0:T(8,128)}, f32[192,128]{1,0:T(8,128)S(1)}, u32[]{:S(2)}, u32[]{:S(2)}) collective-permute-start(f32[192,128]{1,0:T(8,128)} %get-tuple-element.160), channel_id=1, source_target_pairs={{0,8},{4,12},{8,0},{12,4},{1,9},{5,13},{9,1},{13,5},{2,10},{6,14},... | collective-permute-start | bytes 294920 | tf_op jit(solution)/shard_map/cond/branch_0_fun/ppermute | solution.py:46
  207.7 33.3 %collective-permute-start.17 = (bf16[1536,256]{1,0:T(8,128)(2,1)}, bf16[1536,256]{1,0:T(8,128)(2,1)S(1)}, u32[]{:S(2)}, u32[]{:S(2)}) collective-permute-start(bf16[1536,256]{1,0:T(8,128)(2,1)} %stage.19.refs_0_), channel_id=1, source_target_pairs={{0,2},{1,3},{2,0},{3,1},{4,6},{5,7},{6,4},{7,5},{8,10},{9,11},{10,... | collective-permute-start | bytes 2359304 | tf_op jit(solution)/shard_map/cond/branch_0_fun/ppermute | solution.py:46
  227.7 35.6 %collective-permute-start.18 = (bf16[2048,256]{1,0:T(8,128)(2,1)}, bf16[2048,256]{1,0:T(8,128)(2,1)S(1)}, u32[]{:S(2)}, u32[]{:S(2)}) collective-permute-start(bf16[2048,256]{1,0:T(8,128)(2,1)} %get-tuple-element.93.refs_0_.refs_25_), channel_id=1, source_target_pairs={{0,2},{1,3},{2,0},{3,1},{4,6},{5,7},{6,4},{7,5},{8,10},{9,11},{10,... | collective-permute-start | bytes 3145736 | tf_op jit(solution)/shard_map/cond/branch_0_fun/ppermute | solution.py:46
  228.8 6.6 %copy-start.42 = (f32[192,128]{1,0:T(8,128)}, f32[192,128]{1,0:T(8,128)S(1)}, u32[]{:S(2)}) copy-start(f32[192,128]{1,0:T(8,128)S(1)} %collective-permute-done.1.c) | copy-start | bytes 294916 | tf_op jit(solution)/shard_map/cond
  228.8 6.5 %collective-permute-start.2 = (f32[192,128]{1,0:T(8,128)S(1)}, f32[192,128]{1,0:T(8,128)S(1)}, u32[]{:S(2)}, u32[]{:S(2)}) collective-permute-start(f32[192,128]{1,0:T(8,128)S(1)} %get-tuple-element.159), channel_id=1, source_target_pairs={{0,12},{4,8},{8,4},{12,0},{1,13},{5,9},{9,5},{13,1},{2,14},{6,10},... | collective-permute-start | bytes 294920 | tf_op jit(solution)/shard_map/cond/branch_0_fun/ppermute | solution.py:46
  238.4 19.1 %copy-start.29 = (f32[64,128]{1,0:T(8,128)}, f32[64,128]{1,0:T(8,128)S(1)}, u32[]{:S(2)}) copy-start(f32[64,128]{1,0:T(8,128)S(1)} %slice.18.a) | copy-start | bytes 98308 | tf_op jit(solution)/shard_map/cond
  238.4 21.0 %copy-start.17 = (f32[192,128]{1,0:T(8,128)S(1)}, f32[192,128]{1,0:T(8,128)}, u32[]{:S(2)}) copy-start(f32[192,128]{1,0:T(8,128)} %sum_parts.2.refs_26_) | copy-start | bytes 294916 | tf_op jit(solution)/shard_map/cond
  238.4 21.2 %copy-start.34 = (f32[128,256]{1,0:T(8,128)S(1)}, f32[128,256]{1,0:T(8,128)}, u32[]{:S(2)}) copy-start(f32[128,256]{1,0:T(8,128)} %get-tuple-element.95) | copy-start | bytes 393220 | tf_op jit(solution)/shard_map/cond
  238.4 19.1 %collective-permute-start.14 = (f32[64,128]{1,0:T(8,128)S(1)}, f32[64,128]{1,0:T(8,128)S(1)}, u32[]{:S(2)}, u32[]{:S(2)}) collective-permute-start(f32[64,128]{1,0:T(8,128)S(1)} %slice.18.a), channel_id=1, source_target_pairs={{0,4},{4,0},{8,12},{12,8},{1,5},{5,1},{9,13},{13,9},{2,6},{6,2},{1... | collective-permute-start | bytes 98312 | tf_op jit(solution)/shard_map/cond/branch_0_fun/ppermute | solution.py:46
  241.0 20.2 %collective-permute-start.15 = (f32[64,128]{1,0:T(8,128)S(1)}, f32[64,128]{1,0:T(8,128)S(1)}, u32[]{:S(2)}, u32[]{:S(2)}) collective-permute-start(f32[64,128]{1,0:T(8,128)S(1)} %slice.18.a), channel_id=1, source_target_pairs={{0,8},{4,12},{8,0},{12,4},{1,9},{5,13},{9,1},{13,5},{2,10},{6,14},... | collective-permute-start | bytes 98312 | tf_op jit(solution)/shard_map/cond/branch_0_fun/ppermute | solution.py:46
  257.5 5.8 %collective-permute-start.16 = (f32[64,128]{1,0:T(8,128)S(1)}, f32[64,128]{1,0:T(8,128)S(1)}, u32[]{:S(2)}, u32[]{:S(2)}) collective-permute-start(f32[64,128]{1,0:T(8,128)S(1)} %slice.18.a), channel_id=1, source_target_pairs={{0,12},{4,8},{8,4},{12,0},{1,13},{5,9},{9,5},{13,1},{2,14},{6,10},... | collective-permute-start | bytes 98312 | tf_op jit(solution)/shard_map/cond/branch_0_fun/ppermute | solution.py:46
  261.2 23.9 %collective-permute-start.22 = (bf16[1536,256]{1,0:T(8,128)(2,1)}, bf16[1536,256]{1,0:T(8,128)(2,1)S(1)}, u32[]{:S(2)}, u32[]{:S(2)}) collective-permute-start(bf16[1536,256]{1,0:T(8,128)(2,1)} %get-tuple-element.94.refs_0_.refs_25_), channel_id=1, source_target_pairs={{0,2},{1,3},{2,0},{3,1},{4,6},{5,7},{6,4},{7,5},{8,10},{9,11},{10,... | collective-permute-start | bytes 2359304 | tf_op jit(solution)/shard_map/cond/branch_0_fun/ppermute | solution.py:46
  265.8 37.6 %collective-permute-start.19 = (f32[64,512]{1,0:T(8,128)}, f32[64,512]{1,0:T(8,128)S(1)}, u32[]{:S(2)}, u32[]{:S(2)}) collective-permute-start(f32[64,512]{1,0:T(8,128)} %join_parts.2.refs_26_), channel_id=1, source_target_pairs={{0,1},{1,0},{2,3},{3,2},{4,5},{5,4},{6,7},{7,6},{8,9},{9,8},{10,11... | collective-permute-start | bytes 393224 | tf_op jit(solution)/shard_map/cond/branch_0_fun/ppermute | solution.py:46
  284.1 18.3 %copy-start.38 = (f32[128,256]{1,0:T(8,128)S(1)}, f32[128,256]{1,0:T(8,128)}, u32[]{:S(2)}) copy-start(f32[128,256]{1,0:T(8,128)} %get-tuple-element.99) | copy-start | bytes 393220 | tf_op jit(solution)/shard_map/cond
  284.1 19.3 %copy-start.23 = (f32[64,512]{1,0:T(8,128)S(1)}, f32[64,512]{1,0:T(8,128)}, u32[]{:S(2)}) copy-start(f32[64,512]{1,0:T(8,128)} %join_parts.2.refs_26_) | copy-start | bytes 393220 | tf_op jit(solution)/shard_map/cond
  284.1 19.3 %copy-start.53 = (s32[1,1024]{1,0:T(1,128)S(1)}, s32[1,1024]{1,0:T(1,128)}, u32[]{:S(2)}) copy-start(s32[1,1024]{1,0:T(1,128)} %copy-done.52) | copy-start | bytes 12292 | tf_op jit(solution)/shard_map/cond
  284.1 26.2 %collective-permute-start.23 = (bf16[2048,256]{1,0:T(8,128)(2,1)}, bf16[2048,256]{1,0:T(8,128)(2,1)S(1)}, u32[]{:S(2)}, u32[]{:S(2)}) collective-permute-start(bf16[2048,256]{1,0:T(8,128)(2,1)} %get-tuple-element.100.refs_25_), channel_id=1, source_target_pairs={{0,2},{1,3},{2,0},{3,1},{4,6},{5,7},{6,4},{7,5},{8,10},{9,11},{10,... | collective-permute-start | bytes 3145736 | tf_op jit(solution)/shard_map/cond/branch_0_fun/ppermute | solution.py:46
  301.2 25.6 %collective-permute-start.24 = (bf16[1536,256]{1,0:T(8,128)(2,1)}, bf16[1536,256]{1,0:T(8,128)(2,1)S(1)}, u32[]{:S(2)}, u32[]{:S(2)}) collective-permute-start(bf16[1536,256]{1,0:T(8,128)(2,1)} %get-tuple-element.104.refs_17_), channel_id=1, source_target_pairs={{0,2},{1,3},{2,0},{3,1},{4,6},{5,7},{6,4},{7,5},{8,10},{9,11},{10,... | collective-permute-start | bytes 2359304 | tf_op jit(solution)/shard_map/cond/branch_0_fun/ppermute | solution.py:46
  324.7 14.2 %copy-start.8 = (f32[128,256]{1,0:T(8,128)S(1)}, f32[128,256]{1,0:T(8,128)}, u32[]{:S(2)}) copy-start(f32[128,256]{1,0:T(8,128)} %stage.24.refs_17_) | copy-start | bytes 393220 | tf_op jit(solution)/shard_map/cond
  324.7 15.1 %copy-start.32 = (f32[128,256]{1,0:T(8,128)S(1)}, f32[128,256]{1,0:T(8,128)}, u32[]{:S(2)}) copy-start(f32[128,256]{1,0:T(8,128)} %add.173) | copy-start | bytes 393220 | tf_op jit(solution)/shard_map/cond
  324.7 15.1 %copy-start.60 = (f32[64,768]{1,0:T(8,128)S(1)}, f32[64,768]{1,0:T(8,128)}, u32[]{:S(2)}) copy-start(f32[64,768]{1,0:T(8,128)} %fusion.7) | copy-start | bytes 589828 | tf_op jit(solution)/shard_map/cond
  324.7 15.1 %copy-start.61 = (f32[8,768]{1,0:T(8,128)S(1)}, f32[8,768]{1,0:T(8,128)}, u32[]{:S(2)}) copy-start(f32[8,768]{1,0:T(8,128)} %fusion.8) | copy-start | bytes 73732 | tf_op jit(solution)/shard_map/cond
  352.2 6.9 %collective-permute-start.60 = (f32[8,16,192]{2,1,0:T(8,128)S(1)}, f32[8,16,192]{2,1,0:T(8,128)S(1)}, u32[]{:S(2)}, u32[]{:S(2)}) collective-permute-start(f32[8,16,192]{2,1,0:T(8,128)S(1)} %get-tuple-element.171), channel_id=1, source_target_pairs={{0,4},{4,0},{8,12},{12,8},{1,5},{5,1},{9,13},{13,9},{2,6},{6,2},{1... | collective-permute-start | bytes 294920 | tf_op jit(solution)/shard_map/ppermute | solution.py:46
  352.2 12.9 %collective-permute-start.61 = (f32[8,16,192]{2,1,0:T(8,128)S(1)}, f32[8,16,192]{2,1,0:T(8,128)S(1)}, u32[]{:S(2)}, u32[]{:S(2)}) collective-permute-start(f32[8,16,192]{2,1,0:T(8,128)S(1)} %get-tuple-element.173), channel_id=1, source_target_pairs={{0,8},{4,12},{8,0},{12,4},{1,9},{5,13},{9,1},{13,5},{2,10},{6,14},... | collective-permute-start | bytes 294920 | tf_op jit(solution)/shard_map/ppermute | solution.py:46
  354.6 10.5 %collective-permute-start.62 = (f32[8,16,192]{2,1,0:T(8,128)S(1)}, f32[8,16,192]{2,1,0:T(8,128)S(1)}, u32[]{:S(2)}, u32[]{:S(2)}) collective-permute-start(f32[8,16,192]{2,1,0:T(8,128)S(1)} %get-tuple-element.172), channel_id=1, source_target_pairs={{0,12},{4,8},{8,4},{12,0},{1,13},{5,9},{9,5},{13,1},{2,14},{6,10},... | collective-permute-start | bytes 294920 | tf_op jit(solution)/shard_map/ppermute | solution.py:46
  365.2 2.0 collective-permute-start.63
  365.3 6.4 %collective-permute-start.64 = (f32[8,16,192]{2,1,0:T(8,128)S(1)}, f32[8,16,192]{2,1,0:T(8,128)S(1)}, u32[]{:S(2)}, u32[]{:S(2)}) collective-permute-start(f32[8,16,192]{2,1,0:T(8,128)S(1)} %add_add_fusion.1), channel_id=1, source_target_pairs={{0,2},{1,3},{2,0},{3,1},{4,6},{5,7},{6,4},{7,5},{8,10},{9,11},{10,... | collective-permute-start | bytes 294920 | tf_op jit(solution)/shard_map/ppermute | solution.py:46
  366.3 7.2 %collective-permute-start.65 = (f32[8,16,192]{2,1,0:T(8,128)S(1)}, f32[8,16,192]{2,1,0:T(8,128)S(1)}, u32[]{:S(2)}, u32[]{:S(2)}) collective-permute-start(f32[8,16,192]{2,1,0:T(8,128)S(1)} %add_add_fusion.1), channel_id=1, source_target_pairs={{0,3},{1,2},{2,1},{3,0},{4,7},{5,6},{6,5},{7,4},{8,11},{9,10},{10,... | collective-permute-start | bytes 294920 | tf_op jit(solution)/shard_map/ppermute | solution.py:46
  375.5 1.9 collective-permute-start.66
  375.9 3.6 collective-permute-start.67
  376.9 3.0 collective-permute-start.68
  379.9 4.5 %collective-permute-start.69 = (f32[8,128]{1,0:T(8,128)S(1)}, f32[8,128]{1,0:T(8,128)S(1)}, u32[]{:S(2)}, u32[]{:S(2)}) collective-permute-start(f32[8,128]{1,0:T(8,128)S(1)} %add_add_fusion.2), channel_id=1, source_target_pairs={{0,4},{4,0},{8,12},{12,8},{1,5},{5,1},{9,13},{13,9},{2,6},{6,2},{1... | collective-permute-start | bytes 12296 | tf_op jit(solution)/shard_map/ppermute | solution.py:46
  382.0 4.5 %collective-permute-start.70 = (f32[8,128]{1,0:T(8,128)S(1)}, f32[8,128]{1,0:T(8,128)S(1)}, u32[]{:S(2)}, u32[]{:S(2)}) collective-permute-start(f32[8,128]{1,0:T(8,128)S(1)} %add_add_fusion.2), channel_id=1, source_target_pairs={{0,8},{4,12},{8,0},{12,4},{1,9},{5,13},{9,1},{13,5},{2,10},{6,14},... | collective-permute-start | bytes 12296 | tf_op jit(solution)/shard_map/ppermute | solution.py:46
  382.8 5.4 %collective-permute-start.71 = (f32[8,128]{1,0:T(8,128)S(1)}, f32[8,128]{1,0:T(8,128)S(1)}, u32[]{:S(2)}, u32[]{:S(2)}) collective-permute-start(f32[8,128]{1,0:T(8,128)S(1)} %add_add_fusion.2), channel_id=1, source_target_pairs={{0,12},{4,8},{8,4},{12,0},{1,13},{5,9},{9,5},{13,1},{2,14},{6,10},... | collective-permute-start | bytes 12296 | tf_op jit(solution)/shard_map/ppermute | solution.py:46
  (14 other events, 36.3 us)
Sparse Core Ops, SparseCore 0:
  31.7 47.1 all-gather.9
  83.8 50.4 all-gather.7
  135.9 58.2 all-gather.11
